TPU v7x, 256 devices: a whole 4x4x8 slice. The times are simulated.
256 devices in a mesh: rows: 32 (over y_lo, z, core), pairs: 8 (over x, y_hi).
Axes of the slice: x: 4, y: 4 (y_hi: 2, y_lo: 2; y = y_hi * 2 + y_lo), z: 8, core: 2. Of those that a mesh axis runs over, the one named last changes fastest.
Arguments:
- snapshots: float32 [131072, 1024], P('rows', 'pairs'), may hold values from -40 to 40
Outputs:
- rotated_out: float32 [131072, 1024], P('rows', 'pairs')
- column_norms: float32 [1024], P('pairs')
All inputs are finite; a program needn't handle non-finite values.
Results may differ from a plain program's by a relative error of at most 0.0003.
Values sent between devices are 32-bit elements; how exact they have to be, the bound alone decides.
No kernel may reach another device: no remote copies, remote signals or barrier semaphores. Data moves between devices by JAX's collectives and lax.ppermute only.
A program may use at most 64 MiB of HBM per device.

v0:
```python
import jax
import jax.numpy as jnp
from jax import lax
from jax.sharding import PartitionSpec as P

STEPS = 6


HIGH = lax.Precision.HIGHEST


def passed_along(x, axis, by):
    size = lax.axis_size(axis)
    pairs = [(i, i + by) for i in range(size) if 0 <= i + by < size]
    return lax.ppermute(x, axis, pairs)


def rotation(gram):
    size = gram.shape[0]
    diag = jnp.diagonal(gram)
    ratio = gram / (diag[:, None] + diag[None, :])
    row_ids = lax.broadcasted_iota(jnp.int32, (size, size), 0)
    col_ids = lax.broadcasted_iota(jnp.int32, (size, size), 1)
    upper = jnp.where(col_ids > row_ids, ratio, jnp.zeros_like(ratio))
    skew = 0.5 * (upper - upper.T)
    eye = jnp.eye(size, dtype=gram.dtype)
    plus = eye + skew
    system = eye - jnp.dot(skew, skew, precision=HIGH)
    factor = jnp.linalg.cholesky(system)
    right = jnp.dot(plus, plus, precision=HIGH)
    inner = jax.scipy.linalg.solve_triangular(factor, right, lower=True)
    return jax.scipy.linalg.solve_triangular(factor, inner, lower=True, trans=1)


def move_blocks(top_block, top_extra, bottom_block, bottom_extra, place, count):
    first = place == 0
    last = place == count - 1
    send_block = jnp.where(first, bottom_block, top_block)
    send_extra = jnp.where(first, bottom_extra, top_extra)
    got_block, got_extra = passed_along((send_block, send_extra), "pairs", 1)
    back_block, back_extra = passed_along((bottom_block, bottom_extra), "pairs", -1)
    new_top = jnp.where(first, top_block, got_block)
    new_top_extra = jnp.where(first, top_extra, got_extra)
    new_bottom = jnp.where(last, top_block, back_block)
    new_bottom_extra = jnp.where(last, top_extra, back_extra)
    return (new_top, new_top_extra, new_bottom, new_bottom_extra)


def body(snapshots):
    width = snapshots.shape[1] // 2
    place = lax.axis_index("pairs")
    count = lax.axis_size("pairs")
    top_block = snapshots[:, :width]
    bottom_block = snapshots[:, width:]
    top_extra = jnp.zeros((width,), jnp.float32)
    bottom_extra = jnp.zeros((width,), jnp.float32)
    for step in range(STEPS):
        whole = jnp.concatenate([top_block, bottom_block], axis=1)
        local_gram = jnp.einsum(
            "ra,rb->ab", whole, whole, precision=HIGH, preferred_element_type=jnp.float32
        )
        gram = lax.psum(local_gram, "rows")
        turn = rotation(gram)
        rotated = jnp.dot(whole, turn, precision=HIGH, preferred_element_type=jnp.float32)
        image = jnp.dot(gram, turn, precision=HIGH, preferred_element_type=jnp.float32)
        norms = jnp.sqrt(jnp.sum(turn * image, axis=0))
        top_block, top_extra, bottom_block, bottom_extra = move_blocks(
            rotated[:, :width], norms[:width], rotated[:, width:], norms[width:], place, count
        )
    column_norms = jnp.concatenate([top_extra, bottom_extra])
    return (jnp.concatenate([top_block, bottom_block], axis=1), column_norms)


def solution(mesh):
    in_specs = (P("rows", "pairs"),)
    out_specs = (P("rows", "pairs"), P("pairs"))
    return jax.shard_map(body, mesh=mesh, in_specs=in_specs, out_specs=out_specs, check_vma=False)
```

profile of v0, /device:TPU:1, one launch (start us, length us, event | category | flops | bytes accessed | tf_op | source)
XLA Modules:
  0.0 1669.0 jit_solution(9776669041976589895)
XLA Ops:
  7.2 1.5 copy-done
  8.8 4.1 fusion.99
  13.5 192.7 %all-reduce.7.cloned.1.call-done = f32[128,128]{1,0:T(8,128)} async-done(((f32[128,128]{1,0:T(8,128)}), f32[128,128]{1,0:T(8,128)}) %all-reduce.7.cloned.1.call-update) | async-done | bytes 65552 | tf_op jit(solution)/shard_map/psum | solution.py:62
  206.2 1.9 gather_fusion
  209.6 11.7 cholesky.104
  222.6 9.8 custom-call.31
  233.2 1.9 convolution_bitcast_fusion
  235.1 1.3 slice_select_fusion.17
  236.8 5.4 collective-permute-start
  242.1 1.3 collective-permute-start.1
  243.4 41.0 %collective-permute-done = f32[4096,64]{0,1:T(8,128)} collective-permute-done((f32[4096,64]{0,1:T(8,128)}, f32[4096,64]{0,1:T(8,128)}, u32[]{:S(2)}, u32[]{:S(2)}) %collective-permute-start) | collective-permute-done | bytes 1048608 | tf_op jit(solution)/shard_map/ppermute | solution.py:15
  284.5 1.7 slice_select_fusion.16
  286.2 1.0 copy-done.4
  287.2 2.4 fusion.9
  289.8 192.6 %all-reduce.9.cloned.1.call-done = f32[128,128]{1,0:T(8,128)} async-done(((f32[128,128]{1,0:T(8,128)}), f32[128,128]{1,0:T(8,128)}) %all-reduce.9.cloned.1.call-update) | async-done | bytes 65552 | tf_op jit(solution)/shard_map/psum | solution.py:62
  482.4 1.9 gather_fusion.1
  486.0 11.7 cholesky.115
  499.1 9.8 custom-call.33
  509.4 3.2 fusion.8
  512.8 4.4 collective-permute-start.2
  517.2 1.3 collective-permute-start.3
  518.5 41.7 %collective-permute-done.2 = f32[4096,64]{0,1:T(8,128)S(1)} collective-permute-done((f32[4096,64]{0,1:T(8,128)S(1)}, f32[4096,64]{0,1:T(8,128)S(1)}, u32[]{:S(2)}, u32[]{:S(2)}) %collective-permute-start.2) | collective-permute-done | bytes 1048608 | tf_op jit(solution)/shard_map/ppermute | solution.py:15
  561.3 2.4 fusion.7
  564.0 192.2 %all-reduce.11.cloned.1.call-done = f32[128,128]{1,0:T(8,128)} async-done(((f32[128,128]{1,0:T(8,128)}), f32[128,128]{1,0:T(8,128)}) %all-reduce.11.cloned.1.call-update) | async-done | bytes 65552 | tf_op jit(solution)/shard_map/psum | solution.py:62
  756.2 1.9 gather_fusion.2
  759.8 11.7 cholesky.126
  772.9 9.8 custom-call.35
  783.2 3.2 fusion.6
  786.6 4.4 collective-permute-start.4
  791.0 1.3 collective-permute-start.5
  792.3 41.7 %collective-permute-done.4 = f32[4096,64]{0,1:T(8,128)S(1)} collective-permute-done((f32[4096,64]{0,1:T(8,128)S(1)}, f32[4096,64]{0,1:T(8,128)S(1)}, u32[]{:S(2)}, u32[]{:S(2)}) %collective-permute-start.4) | collective-permute-done | bytes 1048608 | tf_op jit(solution)/shard_map/ppermute | solution.py:15
  834.2 1.0 copy-done.3
  835.2 2.4 fusion.5
  838.0 192.0 %all-reduce.13.cloned.1.call-done = f32[128,128]{1,0:T(8,128)} async-done(((f32[128,128]{1,0:T(8,128)}), f32[128,128]{1,0:T(8,128)}) %all-reduce.13.cloned.1.call-update) | async-done | bytes 65552 | tf_op jit(solution)/shard_map/psum | solution.py:62
  1030.1 1.9 gather_fusion.3
  1033.7 11.7 cholesky.137
  1046.7 9.8 custom-call.37
  1057.1 3.2 fusion.4
  1060.4 4.4 collective-permute-start.6
  1064.9 1.3 collective-permute-start.7
  1066.2 41.7 %collective-permute-done.6 = f32[4096,64]{0,1:T(8,128)S(1)} collective-permute-done((f32[4096,64]{0,1:T(8,128)S(1)}, f32[4096,64]{0,1:T(8,128)S(1)}, u32[]{:S(2)}, u32[]{:S(2)}) %collective-permute-start.6) | collective-permute-done | bytes 1048608 | tf_op jit(solution)/shard_map/ppermute | solution.py:15
  1108.0 1.0 copy-done.6
  1109.0 2.4 fusion.3
  1111.7 192.4 %all-reduce.15.cloned.1.call-done = f32[128,128]{1,0:T(8,128)} async-done(((f32[128,128]{1,0:T(8,128)}), f32[128,128]{1,0:T(8,128)}) %all-reduce.15.cloned.1.call-update) | async-done | bytes 65552 | tf_op jit(solution)/shard_map/psum | solution.py:62
  1304.0 1.9 gather_fusion.4
  1307.7 11.7 cholesky.148
  1320.7 9.8 custom-call.39
  1331.0 3.2 fusion.2
  1334.4 4.4 collective-permute-start.8
  1338.8 1.5 collective-permute-start.9
  1340.3 41.5 %collective-permute-done.8 = f32[4096,64]{0,1:T(8,128)S(1)} collective-permute-done((f32[4096,64]{0,1:T(8,128)S(1)}, f32[4096,64]{0,1:T(8,128)S(1)}, u32[]{:S(2)}, u32[]{:S(2)}) %collective-permute-start.8) | collective-permute-done | bytes 1048608 | tf_op jit(solution)/shard_map/ppermute | solution.py:15
  1383.0 2.4 fusion.1
  1385.4 192.5 %all-reduce.17.cloned.1.call-done = f32[128,128]{1,0:T(8,128)} async-done(((f32[128,128]{1,0:T(8,128)}), f32[128,128]{1,0:T(8,128)}) %all-reduce.17.cloned.1.call-update) | async-done | bytes 65552 | tf_op jit(solution)/shard_map/psum | solution.py:62
  1577.9 1.9 gather_fusion.5
  1582.5 11.7 cholesky.159
  1595.6 9.8 custom-call.41
  1605.9 3.2 fusion
  1609.3 4.4 collective-permute-start.10
  1613.7 1.3 collective-permute-start.11
  1615.3 5.5 collective-permute-start.12
  1620.8 1.3 collective-permute-start.13
  1622.1 34.6 %collective-permute-done.12 = f32[64]{0:T(128)S(1)} collective-permute-done((f32[64]{0:T(128)S(1)}, f32[64]{0:T(128)S(1)}, u32[]{:S(2)}, u32[]{:S(2)}) %collective-permute-start.12) | collective-permute-done | bytes 288 | tf_op jit(solution)/shard_map/ppermute | solution.py:15
  1657.6 1.5 pad_maximum_fusion.5
  1659.1 2.9 copy.58
  (118 shorter events, 28.4 us)
Async XLA Ops:
  7.2 1.6 copy-start
  7.2 199.0 %all-reduce.7.cloned.1.call-start = ((), (), s32[]{:S(2)}) async-start(), calls=%async_computation | async-start | bytes 131072 | tf_op jit(solution)/shard_map/psum | solution.py:62
  12.9 469.5 %all-reduce.9.cloned.1.call-start = ((), (), s32[]{:S(2)}) async-start(), calls=%async_computation.1 | async-start | bytes 131072 | tf_op jit(solution)/shard_map/psum | solution.py:62
  235.1 1.7 copy-start.1
  236.8 47.7 %collective-permute-start = (f32[4096,64]{0,1:T(8,128)}, f32[4096,64]{0,1:T(8,128)}, u32[]{:S(2)}, u32[]{:S(2)}) collective-permute-start(f32[4096,64]{0,1:T(8,128)} %get-tuple-element.31), channel_id=1, source_target_pairs={{0,1},{1,2},{2,3},{3,4},{4,5},{5,6},{6,7},{8,9},{9,10},{10,11},{11... | collective-permute-start | bytes 3145736 | tf_op jit(solution)/shard_map/ppermute | solution.py:15
  242.1 42.3 %collective-permute-start.1 = (f32[4096,64]{0,1:T(8,128)S(1)}, f32[4096,64]{0,1:T(8,128)}, u32[]{:S(2)}, u32[]{:S(2)}) collective-permute-start(f32[4096,64]{0,1:T(8,128)S(1)} %get-tuple-element.32), channel_id=1, source_target_pairs={{1,0},{2,1},{3,2},{4,3},{5,4},{6,5},{7,6},{9,8},{10,9},{11,10},{12... | collective-permute-start | bytes 3145736 | tf_op jit(solution)/shard_map/ppermute | solution.py:15
  286.2 1.0 copy-start.4
  289.6 466.6 %all-reduce.11.cloned.1.call-start = ((), (), s32[]{:S(2)}) async-start(), calls=%async_computation.2 | async-start | bytes 131072 | tf_op jit(solution)/shard_map/psum | solution.py:62
  512.8 47.4 %collective-permute-start.2 = (f32[4096,64]{0,1:T(8,128)S(1)}, f32[4096,64]{0,1:T(8,128)S(1)}, u32[]{:S(2)}, u32[]{:S(2)}) collective-permute-start(f32[4096,64]{0,1:T(8,128)S(1)} %get-tuple-element.27), channel_id=1, source_target_pairs={{0,1},{1,2},{2,3},{3,4},{4,5},{5,6},{6,7},{8,9},{9,10},{10,11},{11... | collective-permute-start | bytes 3145736 | tf_op jit(solution)/shard_map/ppermute | solution.py:15
  517.2 43.0 %collective-permute-start.3 = (f32[4096,64]{0,1:T(8,128)S(1)}, f32[4096,64]{0,1:T(8,128)S(1)}, u32[]{:S(2)}, u32[]{:S(2)}) collective-permute-start(f32[4096,64]{0,1:T(8,128)S(1)} %get-tuple-element.28), channel_id=1, source_target_pairs={{1,0},{2,1},{3,2},{4,3},{5,4},{6,5},{7,6},{9,8},{10,9},{11,10},{12... | collective-permute-start | bytes 3145736 | tf_op jit(solution)/shard_map/ppermute | solution.py:15
  560.3 1.0 copy-start.5
  563.8 466.3 %all-reduce.13.cloned.1.call-start = ((), (), s32[]{:S(2)}) async-start(), calls=%async_computation.3 | async-start | bytes 131072 | tf_op jit(solution)/shard_map/psum | solution.py:62
  786.6 47.4 %collective-permute-start.4 = (f32[4096,64]{0,1:T(8,128)S(1)}, f32[4096,64]{0,1:T(8,128)S(1)}, u32[]{:S(2)}, u32[]{:S(2)}) collective-permute-start(f32[4096,64]{0,1:T(8,128)S(1)} %get-tuple-element.23), channel_id=1, source_target_pairs={{0,1},{1,2},{2,3},{3,4},{4,5},{5,6},{6,7},{8,9},{9,10},{10,11},{11... | collective-permute-start | bytes 3145736 | tf_op jit(solution)/shard_map/ppermute | solution.py:15
  791.0 43.0 %collective-permute-start.5 = (f32[4096,64]{0,1:T(8,128)S(1)}, f32[4096,64]{0,1:T(8,128)S(1)}, u32[]{:S(2)}, u32[]{:S(2)}) collective-permute-start(f32[4096,64]{0,1:T(8,128)S(1)} %get-tuple-element.24), channel_id=1, source_target_pairs={{1,0},{2,1},{3,2},{4,3},{5,4},{6,5},{7,6},{9,8},{10,9},{11,10},{12... | collective-permute-start | bytes 3145736 | tf_op jit(solution)/shard_map/ppermute | solution.py:15
  834.2 1.0 copy-start.3
  837.6 466.5 %all-reduce.15.cloned.1.call-start = ((), (), s32[]{:S(2)}) async-start(), calls=%async_computation.4 | async-start | bytes 131072 | tf_op jit(solution)/shard_map/psum | solution.py:62
  1060.4 47.4 %collective-permute-start.6 = (f32[4096,64]{0,1:T(8,128)S(1)}, f32[4096,64]{0,1:T(8,128)S(1)}, u32[]{:S(2)}, u32[]{:S(2)}) collective-permute-start(f32[4096,64]{0,1:T(8,128)S(1)} %get-tuple-element.19), channel_id=1, source_target_pairs={{0,1},{1,2},{2,3},{3,4},{4,5},{5,6},{6,7},{8,9},{9,10},{10,11},{11... | collective-permute-start | bytes 3145736 | tf_op jit(solution)/shard_map/ppermute | solution.py:15
  1064.9 43.0 %collective-permute-start.7 = (f32[4096,64]{0,1:T(8,128)S(1)}, f32[4096,64]{0,1:T(8,128)S(1)}, u32[]{:S(2)}, u32[]{:S(2)}) collective-permute-start(f32[4096,64]{0,1:T(8,128)S(1)} %get-tuple-element.20), channel_id=1, source_target_pairs={{1,0},{2,1},{3,2},{4,3},{5,4},{6,5},{7,6},{9,8},{10,9},{11,10},{12... | collective-permute-start | bytes 3145736 | tf_op jit(solution)/shard_map/ppermute | solution.py:15
  1108.0 1.0 copy-start.6
  1111.4 466.4 %all-reduce.17.cloned.1.call-start = ((), (), s32[]{:S(2)}) async-start(), calls=%async_computation.5 | async-start | bytes 131072 | tf_op jit(solution)/shard_map/psum | solution.py:62
  1334.4 47.4 %collective-permute-start.8 = (f32[4096,64]{0,1:T(8,128)S(1)}, f32[4096,64]{0,1:T(8,128)S(1)}, u32[]{:S(2)}, u32[]{:S(2)}) collective-permute-start(f32[4096,64]{0,1:T(8,128)S(1)} %get-tuple-element.15), channel_id=1, source_target_pairs={{0,1},{1,2},{2,3},{3,4},{4,5},{5,6},{6,7},{8,9},{9,10},{10,11},{11... | collective-permute-start | bytes 3145736 | tf_op jit(solution)/shard_map/ppermute | solution.py:15
  1338.8 43.0 %collective-permute-start.9 = (f32[4096,64]{0,1:T(8,128)S(1)}, f32[4096,64]{0,1:T(8,128)S(1)}, u32[]{:S(2)}, u32[]{:S(2)}) collective-permute-start(f32[4096,64]{0,1:T(8,128)S(1)} %get-tuple-element.16), channel_id=1, source_target_pairs={{1,0},{2,1},{3,2},{4,3},{5,4},{6,5},{7,6},{9,8},{10,9},{11,10},{12... | collective-permute-start | bytes 3145736 | tf_op jit(solution)/shard_map/ppermute | solution.py:15
  1382.0 1.0 copy-start.2
  1609.1 5.9 copy-start.7
  1609.3 48.1 %collective-permute-start.10 = (f32[4096,64]{0,1:T(8,128)S(1)}, f32[4096,64]{0,1:T(8,128)S(1)}, u32[]{:S(2)}, u32[]{:S(2)}) collective-permute-start(f32[4096,64]{0,1:T(8,128)S(1)} %get-tuple-element.11), channel_id=1, source_target_pairs={{0,1},{1,2},{2,3},{3,4},{4,5},{5,6},{6,7},{8,9},{9,10},{10,11},{11... | collective-permute-start | bytes 3145736 | tf_op jit(solution)/shard_map/ppermute | solution.py:15
  1613.7 43.6 %collective-permute-start.11 = (f32[4096,64]{0,1:T(8,128)S(1)}, f32[4096,64]{0,1:T(8,128)S(1)}, u32[]{:S(2)}, u32[]{:S(2)}) collective-permute-start(f32[4096,64]{0,1:T(8,128)S(1)} %get-tuple-element.12), channel_id=1, source_target_pairs={{1,0},{2,1},{3,2},{4,3},{5,4},{6,5},{7,6},{9,8},{10,9},{11,10},{12... | collective-permute-start | bytes 3145736 | tf_op jit(solution)/shard_map/ppermute | solution.py:15
  1615.3 41.4 %collective-permute-start.12 = (f32[64]{0:T(128)S(1)}, f32[64]{0:T(128)S(1)}, u32[]{:S(2)}, u32[]{:S(2)}) collective-permute-start(f32[64]{0:T(128)S(1)} %get-tuple-element.35), channel_id=1, source_target_pairs={{0,1},{1,2},{2,3},{3,4},{4,5},{5,6},{6,7},{8,9},{9,10},{10,11},{11... | collective-permute-start | bytes 776 | tf_op jit(solution)/shard_map/ppermute | solution.py:15
  1620.8 35.9 %collective-permute-start.13 = (f32[64]{0:T(128)S(1)}, f32[64]{0:T(128)S(1)}, u32[]{:S(2)}, u32[]{:S(2)}) collective-permute-start(f32[64]{0:T(128)S(1)} %get-tuple-element.36), channel_id=1, source_target_pairs={{1,0},{2,1},{3,2},{4,3},{5,4},{6,5},{7,6},{9,8},{10,9},{11,10},{12... | collective-permute-start | bytes 776 | tf_op jit(solution)/shard_map/ppermute | solution.py:15
Sparse Core Ops, SparseCore 0:
  13.0 193.1 all-reduce.6
  289.7 192.6 all-reduce.8
  563.9 192.3 all-reduce.10
  837.7 192.3 all-reduce.12
  1111.6 192.4 all-reduce.14
  1385.5 192.3 all-reduce.16
where the time goes:
time: 1680 us; the launch traced here: 1670 us
  waiting for transfers between devices  1400 us (83%)
  other arithmetic  151 us (9%)
  starting transfers between devices  43.9 us (3%)
  matrix products  40.4 us (2%)
  local copies, waits for them, and re-layouts  22.5 us (1%)
    psum x6, waiting for transfers between devices, body(): gram = lax.psum(local_gram, 'rows')  1150 us
    ppermute x14, waiting for transfers between devices, passed_along(): return lax.ppermute(x, axis, pairs)  242 us
    another operation x18, other arithmetic, rotation(): factor = jnp.linalg.cholesky(system)  74.3 us
    another operation x12, other arithmetic, rotation(): return jax.scipy.linalg.solve_triangular(factor, inner, lower=True, trans=1)  62.8 us
    ppermute x14, starting transfers between devices, passed_along(): return lax.ppermute(x, axis, pairs)  42.2 us
  transfers between devices with their start and end apart: 20, of which 12 were waited for; matrix products, arithmetic and copies ran while one was open for 0% of the time, Pallas kernels for 0%

commit v1 on v0

v1 whole, which is shorter than its diff:
```python
import jax
import jax.numpy as jnp
import numpy as np
from jax import lax
from jax.experimental import pallas as pl
from jax.experimental.pallas import tpu as pltpu
from jax.sharding import PartitionSpec as P

STEPS = 6
HALF = 64
WIDE = 2 * HALF
PAIRS = 8
BLOCKS = [(i, j) for i in range(PAIRS) for j in range(i, PAIRS)]
INDEX = {block: t for t, block in enumerate(BLOCKS)}
SHARE = len(BLOCKS) // 2

PAIR_AXES = ("x", "yh")
SUM_AXES = ("yl", "z", "x", "yh")
F32 = jnp.float32
BF16 = jnp.bfloat16
VMEM_LIMIT = 60 * 1024 * 1024

MOVED = {0: 0, 1: 2, 2 * PAIRS - 2: 2 * PAIRS - 1}
for place in range(1, PAIRS - 1):
    MOVED[2 * place] = 2 * (place + 1)
for place in range(1, PAIRS):
    MOVED[2 * place + 1] = 2 * (place - 1) + 1


def split(x):
    high = x.astype(BF16)
    low = (x - high.astype(F32)).astype(BF16)
    return high, low


def left(x):
    return jnp.concatenate(split(x), axis=1)


def right(x):
    both = jnp.concatenate(split(x), axis=1)
    return jnp.concatenate([both, both], axis=0)


def mul(a, b):
    y = jnp.dot(a, b, preferred_element_type=F32)
    n = y.shape[1] // 2
    return y[:, :n] + y[:, n:]


def gram_kernel(x_ref, keep_ref, send_ref, lhs, rhs):
    core = lax.axis_index("c")
    for k in range(PAIRS):
        x = x_ref[k]
        rhs[k] = jnp.concatenate(split(x), axis=1)
        lhs[k] = jnp.concatenate(split(x.T), axis=0)
    for t, (i, j) in enumerate(BLOCKS):
        y = jnp.dot(lhs[i], rhs[j], preferred_element_type=F32)
        y = y[:WIDE] + y[WIDE:]
        y = y[:, :WIDE] + y[:, WIDE:]
        mine = core == t // SHARE

        @pl.when(mine)
        def _():
            keep_ref[t % SHARE] = y

        @pl.when(jnp.logical_not(mine))
        def _():
            send_ref[t % SHARE] = y


def chain_kernel(mine_ref, other_ref, x_ref, y_ref, norms_ref, gram, data, skew, inv, power, turn, turned, norms):
    core = lax.axis_index("c")
    position = lax.axis_index("x") * 2 + lax.axis_index("yh")
    row = lax.broadcasted_iota(jnp.int32, (WIDE, WIDE), 0)
    col = lax.broadcasted_iota(jnp.int32, (WIDE, WIDE), 1)
    eye = (row == col).astype(F32)
    for t in range(len(BLOCKS)):
        gram[0, t] = jnp.where(core == t // SHARE, mine_ref[t % SHARE], other_ref[t % SHARE])
    for k in range(PAIRS):
        data[0, k] = x_ref[k]

    def rotations(now):
        radius = jnp.zeros((1, 1), F32)
        for k in range(PAIRS):
            g = gram[now, INDEX[k, k]]
            diag = g * eye
            total = jnp.sum(diag, axis=0, keepdims=True) + jnp.sum(diag, axis=1, keepdims=True)
            ratio = jnp.clip(0.5 * (g / total), -0.25, 0.25)
            s = jnp.where(col > row, ratio, jnp.where(col < row, -ratio, 0.0))
            skew[k] = s
            square = mul(left(s), right(s))
            bound = jnp.sqrt(0.5 * jnp.sum(square * square, axis=(0, 1), keepdims=True)) * 1.001
            scale = 2.0 / (2.0 + bound)
            power[k] = (1.0 - scale) * eye + scale * square
            inv[k] = scale * (eye + s)
            radius = jnp.maximum(radius, bound / (2.0 + bound))

        def multiply_on(rate):
            for k in range(PAIRS):
                p = inv[k]
                r = power[k]
                y = mul(jnp.concatenate([left(p), left(r)], axis=0), right(r))
                inv[k] = p + y[:WIDE]
                power[k] = y[WIDE:]
            return rate * rate

        lax.while_loop(lambda rate: rate > 5e-5, multiply_on, radius[0, 0])

        def correct(carry):
            rounds, _ = carry
            worst = jnp.zeros((1, 1), F32)
            for k in range(PAIRS):
                p = inv[k]
                e = eye - p + mul(left(skew[k]), right(p))
                inv[k] = p + mul(left(p), right(e))
                worst = jnp.maximum(worst, jnp.sum(e * e, axis=(0, 1), keepdims=True))
            return rounds + 1, worst[0, 0]

        lax.while_loop(lambda c: jnp.logical_and(c[1] > 1e-6, c[0] < 40), correct, (0, jnp.float32(1.0)))

        for k in range(PAIRS):
            j = 2.0 * inv[k] - eye
            turn[k] = right(j)
            turned[k] = left(j.T)

    def put(ref, lead, value, a, b, to_a, to_b):
        part = value[a * HALF : (a + 1) * HALF, :]
        if b != to_b:
            part = pltpu.roll(part, HALF, 1)
        ref[lead + (pl.ds(to_a * HALF, HALF), pl.ds(to_b * HALF, HALF))] = part[:, to_b * HALF : (to_b + 1) * HALF]

    def rotate_gram(now, later):
        for i, j in BLOCKS:
            h = mul(left(gram[now, INDEX[i, j]]), turn[j])
            g = mul(turned[i], right(h))
            flipped = None
            for a in range(2):
                for b in range(2):
                    to_i, to_j = MOVED[2 * i + a], MOVED[2 * j + b]
                    if i == j and a != b and to_i > to_j:
                        continue
                    if to_i <= to_j:
                        put(gram, (later, INDEX[to_i // 2, to_j // 2]), g, a, b, to_i % 2, to_j % 2)
                    if to_i > to_j or (to_i != to_j and to_i // 2 == to_j // 2):
                        if flipped is None:
                            flipped = g.T
                        if to_i > to_j and to_i // 2 != to_j // 2:
                            put(gram, (later, INDEX[to_j // 2, to_i // 2]), flipped, b, a, to_j % 2, to_i % 2)
                        elif to_i > to_j:
                            put(gram, (later, INDEX[to_j // 2, to_i // 2]), flipped, b, a, to_j % 2, to_i % 2)
                            put(gram, (later, INDEX[to_j // 2, to_i // 2]), g, a, b, to_i % 2, to_j % 2)
                        else:
                            put(gram, (later, INDEX[to_i // 2, to_j // 2]), flipped, b, a, to_j % 2, to_i % 2)

    def rotate_data(now, ref, lead):
        for k in range(PAIRS):
            y = mul(left(data[now, k]), turn[k])
            for b in range(2):
                to = MOVED[2 * k + b]
                part = y if b == to % 2 else pltpu.roll(y, HALF, 1)
                side = to % 2 * HALF
                ref[lead + (to // 2, slice(None), pl.ds(side, HALF))] = part[:, side : side + HALF]

    def step(s, carry):
        now = lax.rem(s, 2)
        later = 1 - now
        rotations(now)
        rotate_gram(now, later)
        rotate_data(now, data, (later,))
        return carry

    lax.fori_loop(0, STEPS - 1, step, 0)
    now = (STEPS - 1) % 2
    rotations(now)
    rotate_data(now, y_ref, ())
    for k in range(PAIRS):
        j = 2.0 * inv[k] - eye
        h = mul(left(gram[now, INDEX[k, k]]), turn[k])
        n = jnp.sqrt(jnp.maximum(jnp.sum(j * h, axis=0, keepdims=True), 0.0))
        for b in range(2):
            to = MOVED[2 * k + b]
            part = n if b == to % 2 else pltpu.roll(n, HALF, 1)
            side = to % 2 * HALF
            norms[to // 2, :, pl.ds(side, HALF)] = part[:, side : side + HALF]
    norms_ref[...] = norms[position]


def local_gram(x):
    rows = x.shape[1]
    out = jax.ShapeDtypeStruct((SHARE, WIDE, WIDE), F32)
    return pl.pallas_call(
        gram_kernel,
        out_shape=(out, out),
        scratch_shapes=[
            pltpu.VMEM((PAIRS, 2 * WIDE, rows), BF16),
            pltpu.VMEM((PAIRS, rows, 2 * WIDE), BF16),
        ],
        compiler_params=pltpu.CompilerParams(vmem_limit_bytes=VMEM_LIMIT),
        name="gram",
    )(x)


def chain(mine, other, x):
    rows = x.shape[1]
    square = pltpu.VMEM((PAIRS, WIDE, WIDE), F32)
    return pl.pallas_call(
        chain_kernel,
        out_shape=(
            jax.ShapeDtypeStruct((PAIRS, rows, WIDE), F32),
            jax.ShapeDtypeStruct((1, WIDE), F32),
        ),
        scratch_shapes=[
            pltpu.VMEM((2, len(BLOCKS), WIDE, WIDE), F32),
            pltpu.VMEM((2, PAIRS, rows, WIDE), F32),
            square,
            square,
            square,
            pltpu.VMEM((PAIRS, 2 * WIDE, 2 * WIDE), BF16),
            pltpu.VMEM((PAIRS, WIDE, 2 * WIDE), BF16),
            pltpu.VMEM((PAIRS, 1, WIDE), F32),
        ],
        compiler_params=pltpu.CompilerParams(vmem_limit_bytes=VMEM_LIMIT),
        name="chain",
    )(mine, other, x)


def body(snapshots):
    rows = snapshots.shape[0] // PAIRS
    sharers = lax.axis_size(SUM_AXES)
    x = lax.all_to_all(snapshots, PAIR_AXES, 0, 0, tiled=True).reshape(PAIRS, rows, WIDE)
    keep, send = local_gram(x)
    got = lax.ppermute(send, "c", [(0, 1), (1, 0)])
    part = (keep + got).reshape(sharers, 1, -1)
    part = jnp.sum(lax.all_to_all(part, SUM_AXES, 0, 0, tiled=True), axis=0, keepdims=True)
    part = jnp.broadcast_to(part, (sharers, 1, part.shape[2]))
    mine = lax.all_to_all(part, SUM_AXES, 0, 0, tiled=True).reshape(SHARE, WIDE, WIDE)
    other = lax.ppermute(mine, "c", [(0, 1), (1, 0)])
    y, norms = chain(mine, other, x)
    out = lax.all_to_all(y.reshape(snapshots.shape), PAIR_AXES, 0, 0, tiled=True)
    return out, norms.reshape(WIDE)


def solution(mesh):
    axes = ("yl", "z", "c", "x", "yh")
    finer = jax.sharding.Mesh(mesh.devices.reshape(2, 8, 2, 4, 2), axes)
    rows, pairs = ("yl", "z", "c"), PAIR_AXES
    return jax.shard_map(
        body,
        mesh=finer,
        in_specs=(P(rows, pairs),),
        out_specs=(P(rows, pairs), P(pairs)),
        check_vma=False,
    )
```

time: 1680 us -> 242 us (0.14)
  waiting for transfers between devices: 1400 us -> 5.16 us
  other arithmetic: 151 us -> 2.11 us
  blocking collectives: 0 us -> 146 us
  Pallas kernels: 0 us -> 78.8 us
  matrix products: 40.4 us -> 0 us
  starting transfers between devices: 43.9 us -> 6.39 us
  local copies, waits for them, and re-layouts: 22.5 us -> 2.97 us
    psum x6 -> x0, waiting for transfers between devices: 1150 us -> none  [body(): gram = lax.psum(local_gram, 'rows')]
    ppermute x14 -> x2, waiting for transfers between devices: 242 us -> 5.16 us  [the longest x1 2.68 us: body(): got = lax.ppermute(send, 'c', [(0, 1), (1, 0)])]
    all_to_all x0 -> x4, blocking collectives: none -> 146 us  [the longest x1 43.4 us: body(): lax.all_to_all(part, SUM_AXES, 0, 0, tiled=True)]
    another operation x30 -> x0, other arithmetic: 137 us -> none  [the longest x18 74.3 us: rotation(): factor = jnp.linalg.cholesky(system)]
    pallas_call x0 -> x2, Pallas kernels: none -> 78.8 us  [the longest x1 65.1 us: chain(): pl.pallas_call(chain_kernel, out_shape=(jax.ShapeDtypeStruct((PAIRS, rows...]
    dot_general x25 -> x0, matrix products: 37.5 us -> none  [the longest x6 18.1 us: body(): jnp.dot(whole, turn, precision=HIGH, preferred_element_type=jnp.float32)]
    ppermute x14 -> x2, starting transfers between devices: 42.2 us -> 6.39 us  [the longest x1 3.91 us: body(): other = lax.ppermute(mine, 'c', [(0, 1), (1, 0)])]
  transfers between devices with their start and end apart: 20 -> 2, of which waited for: 12 -> 2; matrix products, arithmetic and copies ran while one was open for 0% -> 0% of each run, Pallas kernels for 0% -> 0%
where the time goes in v1:
time: 242 us
  blocking collectives  146 us (60%)
  Pallas kernels  78.8 us (33%)
  starting transfers between devices  6.39 us (3%)
  waiting for transfers between devices  5.16 us (2%)
  local copies, waits for them, and re-layouts  2.97 us (1%)
    pallas_call x1, Pallas kernels, chain(): pl.pallas_call(chain_kernel, out_shape=(jax.ShapeDtypeStruct((PAIRS, rows...  65.1 us
    all_to_all x1, blocking collectives, body(): lax.all_to_all(part, SUM_AXES, 0, 0, tiled=True)  43.4 us
    all_to_all x1, blocking collectives, body(): lax.all_to_all(part, SUM_AXES, 0, 0, tiled=True).reshape(SHARE, WIDE, WIDE)  37.7 us
    all_to_all x1, blocking collectives, body(): lax.all_to_all(snapshots, PAIR_AXES, 0, 0, tiled=True)  34.2 us
    all_to_all x1, blocking collectives, body(): lax.all_to_all(y.reshape(snapshots.shape), PAIR_AXES, 0, 0, tiled=True)  30.5 us
    pallas_call x1, Pallas kernels, local_gram(): pl.pallas_call(gram_kernel, out_shape=(out, out), scratch_shapes=[pltpu.V...  13.6 us
  transfers between devices with their start and end apart: 2, of which 2 were waited for; matrix products, arithmetic and copies ran while one was open for 0% of the time, Pallas kernels for 0%

profile of v1, /device:TPU:1, one launch (start us, length us, event | category | flops | bytes accessed | tf_op | source)
XLA Modules:
  0.0 241.8 jit_solution(13181018074926488973)
XLA Ops:
  0.6 34.2 %all_to_all.28.x_ref = f32[8,512,128]{2,1,0:T(8,128)} all-to-all(f32[8,512,128]{2,1,0:T(8,128)} %bitcast.9), channel_id=1, replica_groups=mesh['yl'=2,'z'=8,'c'=2,'x'=4,'yh'=2] {'x','yh'}, dimensions={0} | all-to-all | bytes 4194304 | tf_op jit(solution)/shard_map/all_to_all | solution.py:231
  34.8 13.6 %gram.1 = (f32[18,128,128]{2,1,0:T(8,128)}, f32[18,128,128]{2,1,0:T(8,128)}) custom-call(f32[8,512,128]{2,1,0:T(8,128)} %all_to_all.28.x_ref), custom_call_target="tpu_custom_call" | custom-call | tf_op jit(solution)/shard_map/gram/pallas_call | solution.py:192
  48.4 2.5 %collective-permute-start = (f32[18,128,128]{2,1,0:T(8,128)}, f32[18,128,128]{2,1,0:T(8,128)S(1)}, u32[]{:S(2)}, u32[]{:S(2)}) collective-permute-start(f32[18,128,128]{2,1,0:T(8,128)} %get-tuple-element.7), channel_id=1, source_target_pairs={{0,8},{8,0},{1,9},{9,1},{2,10},{10,2},{3,11},{11,3},{4,12},{12,4},... | collective-permute-start | bytes 3538952 | tf_op jit(solution)/shard_map/ppermute | solution.py:233
  50.9 2.7 %collective-permute-done = f32[18,128,128]{2,1,0:T(8,128)S(1)} collective-permute-done((f32[18,128,128]{2,1,0:T(8,128)}, f32[18,128,128]{2,1,0:T(8,128)S(1)}, u32[]{:S(2)}, u32[]{:S(2)}) %collective-permute-start) | collective-permute-done | bytes 1179680 | tf_op jit(solution)/shard_map/ppermute | solution.py:233
  53.6 1.4 add.3
  55.0 43.4 %all_to_all.29 = f32[128,1,2304]{2,1,0:T(1,128)S(1)} all-to-all(f32[128,1,2304]{2,1,0:T(1,128)S(1)} %bitcast.6), channel_id=1, replica_groups=mesh['yl'=2,'z'=8,'c'=2,'x'=4,'yh'=2] {'yl','z','x','yh'}, dimensions={0} | all-to-all | bytes 2359296 | tf_op jit(solution)/shard_map/all_to_all | solution.py:235
  98.5 0.7 reduce_sum.9
  99.1 0.6 broadcast_in_dim.2
  99.8 37.7 %all_to_all.30 = f32[128,1,2304]{2,1,0:T(1,128)S(1)} all-to-all(f32[128,1,2304]{2,1,0:T(1,128)S(1)} %broadcast_in_dim.2), channel_id=1, replica_groups=mesh['yl'=2,'z'=8,'c'=2,'x'=4,'yh'=2] {'yl','z','x','yh'}, dimensions={0} | all-to-all | bytes 2359296 | tf_op jit(solution)/shard_map/all_to_all | solution.py:237
  137.5 0.0 copy-start
  137.5 3.9 %collective-permute-start.1 = (f32[18,128,128]{2,1,0:T(8,128)S(1)}, f32[18,128,128]{2,1,0:T(8,128)S(1)}, u32[]{:S(2)}, u32[]{:S(2)}) collective-permute-start(f32[18,128,128]{2,1,0:T(8,128)S(1)} %bitcast.7), channel_id=1, source_target_pairs={{0,8},{8,0},{1,9},{9,1},{2,10},{10,2},{3,11},{11,3},{4,12},{12,4},... | collective-permute-start | bytes 3538952 | tf_op jit(solution)/shard_map/ppermute | solution.py:238
  141.4 2.5 %collective-permute-done.1.other_ref = f32[18,128,128]{2,1,0:T(8,128)S(1)} collective-permute-done((f32[18,128,128]{2,1,0:T(8,128)S(1)}, f32[18,128,128]{2,1,0:T(8,128)S(1)}, u32[]{:S(2)}, u32[]{:S(2)}) %collective-permute-start.1) | collective-permute-done | bytes 1179680 | tf_op jit(solution)/shard_map/ppermute | solution.py:238
  143.9 0.0 copy-done
  143.9 0.0 copy-start.1
  143.9 1.0 copy-done.1
  144.9 65.1 %chain.1 = (f32[8,512,128]{2,1,0:T(8,128)}, f32[1,128]{1,0:T(1,128)}) custom-call(f32[18,128,128]{2,1,0:T(8,128)} %bitcast.8, f32[18,128,128]{2,1,0:T(8,128)} %copy-done.1, f32[8,512,128]{2,1,0:T(8,128)} %all_to_all.28.x_ref), custom_call_target="tpu_custom_call" | custom-call | tf_op jit(solution)/shard_map/chain/pallas_call | solution.py:207
  210.0 30.5 %all_to_all.31 = f32[8,512,128]{2,1,0:T(8,128)S(1)} all-to-all(f32[8,512,128]{2,1,0:T(8,128)} %get-tuple-element.8), channel_id=1, replica_groups=mesh['yl'=2,'z'=8,'c'=2,'x'=4,'yh'=2] {'x','yh'}, dimensions={0} | all-to-all | bytes 4194304 | tf_op jit(solution)/shard_map/all_to_all | solution.py:240
  240.5 1.3 copy.5
Async XLA Ops:
  48.4 5.2 %collective-permute-start = (f32[18,128,128]{2,1,0:T(8,128)}, f32[18,128,128]{2,1,0:T(8,128)S(1)}, u32[]{:S(2)}, u32[]{:S(2)}) collective-permute-start(f32[18,128,128]{2,1,0:T(8,128)} %get-tuple-element.7), channel_id=1, source_target_pairs={{0,8},{8,0},{1,9},{9,1},{2,10},{10,2},{3,11},{11,3},{4,12},{12,4},... | collective-permute-start | bytes 3538952 | tf_op jit(solution)/shard_map/ppermute | solution.py:233
  137.5 6.4 %copy-start = (f32[128,1,2304]{2,1,0:T(1,128)}, f32[128,1,2304]{2,1,0:T(1,128)S(1)}, u32[]{:S(2)}) copy-start(f32[128,1,2304]{2,1,0:T(1,128)S(1)} %all_to_all.30) | copy-start | bytes 3538948
  137.5 6.4 %collective-permute-start.1 = (f32[18,128,128]{2,1,0:T(8,128)S(1)}, f32[18,128,128]{2,1,0:T(8,128)S(1)}, u32[]{:S(2)}, u32[]{:S(2)}) collective-permute-start(f32[18,128,128]{2,1,0:T(8,128)S(1)} %bitcast.7), channel_id=1, source_target_pairs={{0,8},{8,0},{1,9},{9,1},{2,10},{10,2},{3,11},{11,3},{4,12},{12,4},... | collective-permute-start | bytes 3538952 | tf_op jit(solution)/shard_map/ppermute | solution.py:238
  143.9 1.0 copy-start.1

commit v2 on v1

--- a/solution.py
+++ b/solution.py
@@ -27,23 +27,49 @@
     MOVED[2 * place + 1] = 2 * (place - 1) + 1
 
 
+def sources(block):
+    return [next(t for t, u in MOVED.items() if u == b) for b in block]
+
+
+def updates():
+    lists = []
+    needed = {(2 * k + a, 2 * k + b) for k in range(PAIRS) for a in range(2) for b in range(a, 2)}
+    inside = set(needed)
+    for _ in range(STEPS - 1):
+        blocks = set()
+        for block in needed:
+            old = sorted(sources(block))
+            blocks.add((old[0] // 2, old[1] // 2))
+        lists.insert(0, sorted(blocks))
+        needed = set(inside)
+        for i, j in blocks:
+            needed |= {tuple(sorted((2 * i + a, 2 * j + b))) for a in range(2) for b in range(2)}
+    return lists
+
+
+KMODE = True
+
+
 def split(x):
     high = x.astype(BF16)
     low = (x - high.astype(F32)).astype(BF16)
     return high, low
 
 
-def left(x):
-    return jnp.concatenate(split(x), axis=1)
-
-
-def right(x):
+def left(x, k=None):
+    return jnp.concatenate(split(x), axis=1 if (KMODE if k is None else k) else 0)
+
+
+def right(x, k=None):
     both = jnp.concatenate(split(x), axis=1)
-    return jnp.concatenate([both, both], axis=0)
-
-
-def mul(a, b):
+    return jnp.concatenate([both, both], axis=0) if (KMODE if k is None else k) else both
+
+
+def mul(a, b, k=None):
     y = jnp.dot(a, b, preferred_element_type=F32)
+    if not (KMODE if k is None else k):
+        m = y.shape[0] // 2
+        y = y[:m] + y[m:]
     n = y.shape[1] // 2
     return y[:, :n] + y[:, n:]
 
@@ -54,36 +80,32 @@
         x = x_ref[k]
         rhs[k] = jnp.concatenate(split(x), axis=1)
         lhs[k] = jnp.concatenate(split(x.T), axis=0)
-    for t, (i, j) in enumerate(BLOCKS):
+
+    def block(i, j):
         y = jnp.dot(lhs[i], rhs[j], preferred_element_type=F32)
         y = y[:WIDE] + y[WIDE:]
-        y = y[:, :WIDE] + y[:, WIDE:]
-        mine = core == t // SHARE
-
-        @pl.when(mine)
-        def _():
-            keep_ref[t % SHARE] = y
-
-        @pl.when(jnp.logical_not(mine))
-        def _():
-            send_ref[t % SHARE] = y
-
-
-def chain_kernel(mine_ref, other_ref, x_ref, y_ref, norms_ref, gram, data, skew, inv, power, turn, turned, norms):
+        return y[:, :WIDE] + y[:, WIDE:]
+
+    for t in range(SHARE):
+        first = block(*BLOCKS[t])
+        second = block(*BLOCKS[t + SHARE])
+        keep_ref[t] = jnp.where(core == 0, first, second)
+        send_ref[t] = jnp.where(core == 0, second, first)
+
+
+def chain_kernel(mine_ref, other_ref, x_ref, y_ref, norms_ref, gram, half, data, data_left, skew, inv, power, turn, turned, norms):
     core = lax.axis_index("c")
     position = lax.axis_index("x") * 2 + lax.axis_index("yh")
     row = lax.broadcasted_iota(jnp.int32, (WIDE, WIDE), 0)
     col = lax.broadcasted_iota(jnp.int32, (WIDE, WIDE), 1)
     eye = (row == col).astype(F32)
     for t in range(len(BLOCKS)):
-        gram[0, t] = jnp.where(core == t // SHARE, mine_ref[t % SHARE], other_ref[t % SHARE])
-    for k in range(PAIRS):
-        data[0, k] = x_ref[k]
-
-    def rotations(now):
+        gram[t] = jnp.where(core == t // SHARE, mine_ref[t % SHARE], other_ref[t % SHARE])
+
+    def rotations():
         radius = jnp.zeros((1, 1), F32)
         for k in range(PAIRS):
-            g = gram[now, INDEX[k, k]]
+            g = gram[INDEX[k, k]]
             diag = g * eye
             total = jnp.sum(diag, axis=0, keepdims=True) + jnp.sum(diag, axis=1, keepdims=True)
             ratio = jnp.clip(0.5 * (g / total), -0.25, 0.25)
@@ -100,12 +122,12 @@
             for k in range(PAIRS):
                 p = inv[k]
                 r = power[k]
-                y = mul(jnp.concatenate([left(p), left(r)], axis=0), right(r))
+                y = mul(jnp.concatenate([left(p, True), left(r, True)], axis=0), right(r, True), True)
                 inv[k] = p + y[:WIDE]
                 power[k] = y[WIDE:]
             return rate * rate
 
-        lax.while_loop(lambda rate: rate > 5e-5, multiply_on, radius[0, 0])
+        lax.while_loop(lambda rate: rate > 2e-3, multiply_on, radius[0, 0])
 
         def correct(carry):
             rounds, _ = carry
@@ -117,7 +139,7 @@
                 worst = jnp.maximum(worst, jnp.sum(e * e, axis=(0, 1), keepdims=True))
             return rounds + 1, worst[0, 0]
 
-        lax.while_loop(lambda c: jnp.logical_and(c[1] > 1e-6, c[0] < 40), correct, (0, jnp.float32(1.0)))
+        lax.while_loop(lambda c: jnp.logical_and(c[1] > 3e-5, c[0] < 40), correct, (0, jnp.float32(1.0)))
 
         for k in range(PAIRS):
             j = 2.0 * inv[k] - eye
@@ -128,55 +150,74 @@
         part = value[a * HALF : (a + 1) * HALF, :]
         if b != to_b:
             part = pltpu.roll(part, HALF, 1)
-        ref[lead + (pl.ds(to_a * HALF, HALF), pl.ds(to_b * HALF, HALF))] = part[:, to_b * HALF : (to_b + 1) * HALF]
-
-    def rotate_gram(now, later):
-        for i, j in BLOCKS:
-            h = mul(left(gram[now, INDEX[i, j]]), turn[j])
-            g = mul(turned[i], right(h))
+        ref[lead, pl.ds(to_a * HALF, HALF), pl.ds(to_b * HALF, HALF)] = part[:, to_b * HALF : (to_b + 1) * HALF]
+
+    def rotate_gram(blocks):
+        for i, j in blocks:
+            half[INDEX[i, j]] = right(mul(left(gram[INDEX[i, j]]), turn[j]), False)
+        for i, j in blocks:
+            h = half[INDEX[i, j]]
+            g = mul(turned[i], jnp.concatenate([h, h], axis=0) if KMODE else h)
             flipped = None
             for a in range(2):
                 for b in range(2):
                     to_i, to_j = MOVED[2 * i + a], MOVED[2 * j + b]
                     if i == j and a != b and to_i > to_j:
                         continue
-                    if to_i <= to_j:
-                        put(gram, (later, INDEX[to_i // 2, to_j // 2]), g, a, b, to_i % 2, to_j % 2)
-                    if to_i > to_j or (to_i != to_j and to_i // 2 == to_j // 2):
-                        if flipped is None:
-                            flipped = g.T
-                        if to_i > to_j and to_i // 2 != to_j // 2:
-                            put(gram, (later, INDEX[to_j // 2, to_i // 2]), flipped, b, a, to_j % 2, to_i % 2)
-                        elif to_i > to_j:
-                            put(gram, (later, INDEX[to_j // 2, to_i // 2]), flipped, b, a, to_j % 2, to_i % 2)
-                            put(gram, (later, INDEX[to_j // 2, to_i // 2]), g, a, b, to_i % 2, to_j % 2)
-                        else:
-                            put(gram, (later, INDEX[to_i // 2, to_j // 2]), flipped, b, a, to_j % 2, to_i % 2)
-
-    def rotate_data(now, ref, lead):
+                    low, high = min(to_i, to_j), max(to_i, to_j)
+                    target = INDEX[low // 2, high // 2]
+                    within = low // 2 == high // 2 and low != high
+                    if to_i <= to_j or within:
+                        put(gram, target, g, a, b, to_i % 2, to_j % 2)
+                    if to_i > to_j or within:
+                        flipped = g.T if flipped is None else flipped
+                        put(gram, target, flipped, b, a, to_j % 2, to_i % 2)
+
+    def moved(k, top, bottom):
+        sides = []
+        for side in range(2):
+            (source,) = sources([2 * k + side])
+            value = data[source // 2]
+            sides.append(value if source % 2 == side else pltpu.roll(value, HALF, 1))
+        lane = lax.broadcasted_iota(jnp.int32, sides[0].shape, 1)
+        return jnp.where(lane < HALF, sides[0], sides[1])
+
+    def rotate_data(s):
+        @pl.when(s == 0)
+        def _():
+            for k in range(PAIRS):
+                data_left[k] = left(x_ref[k])
+
+        @pl.when(s > 0)
+        def _():
+            for k in range(PAIRS):
+                data_left[k] = left(moved(k, 0, 0))
+
         for k in range(PAIRS):
-            y = mul(left(data[now, k]), turn[k])
-            for b in range(2):
-                to = MOVED[2 * k + b]
-                part = y if b == to % 2 else pltpu.roll(y, HALF, 1)
-                side = to % 2 * HALF
-                ref[lead + (to // 2, slice(None), pl.ds(side, HALF))] = part[:, side : side + HALF]
+            data[k] = mul(data_left[k], turn[k])
+
+    lists = updates()
 
     def step(s, carry):
-        now = lax.rem(s, 2)
-        later = 1 - now
-        rotations(now)
-        rotate_gram(now, later)
-        rotate_data(now, data, (later,))
+        rotations()
+        for first in range(STEPS - 1):
+            if first and lists[first] == lists[first - 1]:
+                continue
+            steps = [t for t in range(STEPS - 1) if lists[t] == lists[first]]
+
+            @pl.when(jnp.logical_and(s >= steps[0], s <= steps[-1]))
+            def _():
+                rotate_gram(lists[first])
+
+        rotate_data(s)
         return carry
 
-    lax.fori_loop(0, STEPS - 1, step, 0)
-    now = (STEPS - 1) % 2
-    rotations(now)
-    rotate_data(now, y_ref, ())
+    lax.fori_loop(0, STEPS, step, 0)
+    for k in range(PAIRS):
+        y_ref[k] = moved(k, 0, 0)
     for k in range(PAIRS):
         j = 2.0 * inv[k] - eye
-        h = mul(left(gram[now, INDEX[k, k]]), turn[k])
+        h = mul(left(gram[INDEX[k, k]]), turn[k])
         n = jnp.sqrt(jnp.maximum(jnp.sum(j * h, axis=0, keepdims=True), 0.0))
         for b in range(2):
             to = MOVED[2 * k + b]
@@ -211,13 +252,15 @@
             jax.ShapeDtypeStruct((1, WIDE), F32),
         ),
         scratch_shapes=[
-            pltpu.VMEM((2, len(BLOCKS), WIDE, WIDE), F32),
-            pltpu.VMEM((2, PAIRS, rows, WIDE), F32),
+            pltpu.VMEM((len(BLOCKS), WIDE, WIDE), F32),
+            pltpu.VMEM((len(BLOCKS), WIDE, 2 * WIDE), BF16),
+            pltpu.VMEM((PAIRS, rows, WIDE), F32),
+            pltpu.VMEM((PAIRS, rows, 2 * WIDE) if KMODE else (PAIRS, 2 * rows, WIDE), BF16),
             square,
             square,
             square,
-            pltpu.VMEM((PAIRS, 2 * WIDE, 2 * WIDE), BF16),
-            pltpu.VMEM((PAIRS, WIDE, 2 * WIDE), BF16),
+            pltpu.VMEM((PAIRS, 2 * WIDE, 2 * WIDE) if KMODE else (PAIRS, WIDE, 2 * WIDE), BF16),
+            pltpu.VMEM((PAIRS, WIDE, 2 * WIDE) if KMODE else (PAIRS, 2 * WIDE, WIDE), BF16),
             pltpu.VMEM((PAIRS, 1, WIDE), F32),
         ],
         compiler_params=pltpu.CompilerParams(vmem_limit_bytes=VMEM_LIMIT),

time: 242 us -> 216 us (0.89)
  Pallas kernels: 78.8 us -> 52.8 us
    pallas_call x1, Pallas kernels: 65.1 us -> 47.1 us  [chain(): pl.pallas_call(chain_kernel, out_shape=(jax.ShapeDtypeStruct((PAIRS, rows...]
    pallas_call x1, Pallas kernels: 13.6 us -> 5.71 us  [local_gram(): pl.pallas_call(gram_kernel, out_shape=(out, out), scratch_shapes=[pltpu.V...]
where the time goes in v2:
time: 216 us
  blocking collectives  146 us (68%)
  Pallas kernels  52.8 us (24%)
  starting transfers between devices  6.39 us (3%)
  waiting for transfers between devices  5.16 us (2%)
  local copies, waits for them, and re-layouts  2.97 us (1%)
    pallas_call x1, Pallas kernels, chain(): pl.pallas_call(chain_kernel, out_shape=(jax.ShapeDtypeStruct((PAIRS, rows...  47.1 us
    all_to_all x1, blocking collectives, body(): lax.all_to_all(part, SUM_AXES, 0, 0, tiled=True)  43.4 us
    all_to_all x1, blocking collectives, body(): lax.all_to_all(part, SUM_AXES, 0, 0, tiled=True).reshape(SHARE, WIDE, WIDE)  37.7 us
    all_to_all x1, blocking collectives, body(): lax.all_to_all(snapshots, PAIR_AXES, 0, 0, tiled=True)  34.2 us
    all_to_all x1, blocking collectives, body(): lax.all_to_all(y.reshape(snapshots.shape), PAIR_AXES, 0, 0, tiled=True)  30.5 us
    pallas_call x1, Pallas kernels, local_gram(): pl.pallas_call(gram_kernel, out_shape=(out, out), scratch_shapes=[pltpu.V...  5.71 us
  transfers between devices with their start and end apart: 2, of which 2 were waited for; matrix products, arithmetic and copies ran while one was open for 0% of the time, Pallas kernels for 0%

profile of v2, /device:TPU:1, one launch (start us, length us, event | category | flops | bytes accessed | tf_op | source)
XLA Modules:
  0.0 215.8 jit_solution(5227707566089551780)
XLA Ops:
  0.6 34.2 %all_to_all.28.x_ref = f32[8,512,128]{2,1,0:T(8,128)} all-to-all(f32[8,512,128]{2,1,0:T(8,128)} %bitcast.9), channel_id=1, replica_groups=mesh['yl'=2,'z'=8,'c'=2,'x'=4,'yh'=2] {'x','yh'}, dimensions={0} | all-to-all | bytes 4194304 | tf_op jit(solution)/shard_map/all_to_all | solution.py:274
  34.8 5.7 %gram.1 = (f32[18,128,128]{2,1,0:T(8,128)}, f32[18,128,128]{2,1,0:T(8,128)}) custom-call(f32[8,512,128]{2,1,0:T(8,128)} %all_to_all.28.x_ref), custom_call_target="tpu_custom_call" | custom-call | tf_op jit(solution)/shard_map/gram/pallas_call | solution.py:233
  40.5 2.5 %collective-permute-start = (f32[18,128,128]{2,1,0:T(8,128)}, f32[18,128,128]{2,1,0:T(8,128)S(1)}, u32[]{:S(2)}, u32[]{:S(2)}) collective-permute-start(f32[18,128,128]{2,1,0:T(8,128)} %get-tuple-element.7), channel_id=1, source_target_pairs={{0,8},{8,0},{1,9},{9,1},{2,10},{10,2},{3,11},{11,3},{4,12},{12,4},... | collective-permute-start | bytes 3538952 | tf_op jit(solution)/shard_map/ppermute | solution.py:276
  43.0 2.7 %collective-permute-done = f32[18,128,128]{2,1,0:T(8,128)S(1)} collective-permute-done((f32[18,128,128]{2,1,0:T(8,128)}, f32[18,128,128]{2,1,0:T(8,128)S(1)}, u32[]{:S(2)}, u32[]{:S(2)}) %collective-permute-start) | collective-permute-done | bytes 1179680 | tf_op jit(solution)/shard_map/ppermute | solution.py:276
  45.7 1.4 add.3
  47.1 43.4 %all_to_all.29 = f32[128,1,2304]{2,1,0:T(1,128)S(1)} all-to-all(f32[128,1,2304]{2,1,0:T(1,128)S(1)} %bitcast.6), channel_id=1, replica_groups=mesh['yl'=2,'z'=8,'c'=2,'x'=4,'yh'=2] {'yl','z','x','yh'}, dimensions={0} | all-to-all | bytes 2359296 | tf_op jit(solution)/shard_map/all_to_all | solution.py:278
  90.5 0.7 reduce_sum.9
  91.2 0.6 broadcast_in_dim.2
  91.8 37.7 %all_to_all.30 = f32[128,1,2304]{2,1,0:T(1,128)S(1)} all-to-all(f32[128,1,2304]{2,1,0:T(1,128)S(1)} %broadcast_in_dim.2), channel_id=1, replica_groups=mesh['yl'=2,'z'=8,'c'=2,'x'=4,'yh'=2] {'yl','z','x','yh'}, dimensions={0} | all-to-all | bytes 2359296 | tf_op jit(solution)/shard_map/all_to_all | solution.py:280
  129.5 0.0 copy-start
  129.5 3.9 %collective-permute-start.1 = (f32[18,128,128]{2,1,0:T(8,128)S(1)}, f32[18,128,128]{2,1,0:T(8,128)S(1)}, u32[]{:S(2)}, u32[]{:S(2)}) collective-permute-start(f32[18,128,128]{2,1,0:T(8,128)S(1)} %bitcast.7), channel_id=1, source_target_pairs={{0,8},{8,0},{1,9},{9,1},{2,10},{10,2},{3,11},{11,3},{4,12},{12,4},... | collective-permute-start | bytes 3538952 | tf_op jit(solution)/shard_map/ppermute | solution.py:281
  133.5 2.5 %collective-permute-done.1.other_ref = f32[18,128,128]{2,1,0:T(8,128)S(1)} collective-permute-done((f32[18,128,128]{2,1,0:T(8,128)S(1)}, f32[18,128,128]{2,1,0:T(8,128)S(1)}, u32[]{:S(2)}, u32[]{:S(2)}) %collective-permute-start.1) | collective-permute-done | bytes 1179680 | tf_op jit(solution)/shard_map/ppermute | solution.py:281
  135.9 0.0 copy-done
  135.9 0.0 copy-start.1
  135.9 1.0 copy-done.1
  137.0 47.1 %chain.1 = (f32[8,512,128]{2,1,0:T(8,128)}, f32[1,128]{1,0:T(1,128)}) custom-call(f32[18,128,128]{2,1,0:T(8,128)} %bitcast.8, f32[18,128,128]{2,1,0:T(8,128)} %copy-done.1, f32[8,512,128]{2,1,0:T(8,128)} %all_to_all.28.x_ref), custom_call_target="tpu_custom_call" | custom-call | tf_op jit(solution)/shard_map/chain/pallas_call | solution.py:248
  184.0 30.5 %all_to_all.31 = f32[8,512,128]{2,1,0:T(8,128)S(1)} all-to-all(f32[8,512,128]{2,1,0:T(8,128)} %get-tuple-element.8), channel_id=1, replica_groups=mesh['yl'=2,'z'=8,'c'=2,'x'=4,'yh'=2] {'x','yh'}, dimensions={0} | all-to-all | bytes 4194304 | tf_op jit(solution)/shard_map/all_to_all | solution.py:283
  214.5 1.3 copy.5
Async XLA Ops:
  40.5 5.2 %collective-permute-start = (f32[18,128,128]{2,1,0:T(8,128)}, f32[18,128,128]{2,1,0:T(8,128)S(1)}, u32[]{:S(2)}, u32[]{:S(2)}) collective-permute-start(f32[18,128,128]{2,1,0:T(8,128)} %get-tuple-element.7), channel_id=1, source_target_pairs={{0,8},{8,0},{1,9},{9,1},{2,10},{10,2},{3,11},{11,3},{4,12},{12,4},... | collective-permute-start | bytes 3538952 | tf_op jit(solution)/shard_map/ppermute | solution.py:276
  129.5 6.4 %copy-start = (f32[128,1,2304]{2,1,0:T(1,128)}, f32[128,1,2304]{2,1,0:T(1,128)S(1)}, u32[]{:S(2)}) copy-start(f32[128,1,2304]{2,1,0:T(1,128)S(1)} %all_to_all.30) | copy-start | bytes 3538948
  129.5 6.4 %collective-permute-start.1 = (f32[18,128,128]{2,1,0:T(8,128)S(1)}, f32[18,128,128]{2,1,0:T(8,128)S(1)}, u32[]{:S(2)}, u32[]{:S(2)}) collective-permute-start(f32[18,128,128]{2,1,0:T(8,128)S(1)} %bitcast.7), channel_id=1, source_target_pairs={{0,8},{8,0},{1,9},{9,1},{2,10},{10,2},{3,11},{11,3},{4,12},{12,4},... | collective-permute-start | bytes 3538952 | tf_op jit(solution)/shard_map/ppermute | solution.py:281
  135.9 1.0 copy-start.1

commit v3 on v2

--- a/solution.py
+++ b/solution.py
@@ -15,7 +15,7 @@
 SHARE = len(BLOCKS) // 2
 
 PAIR_AXES = ("x", "yh")
-SUM_AXES = ("yl", "z", "x", "yh")
+PLANE_AXES = ("yl", "x", "yh")
 F32 = jnp.float32
 BF16 = jnp.bfloat16
 VMEM_LIMIT = 60 * 1024 * 1024
@@ -268,17 +268,22 @@
     )(mine, other, x)
 
 
+def swapped(x, axis, by):
+    return lax.ppermute(x, axis, [(i, i ^ by) for i in range(lax.axis_size(axis))])
+
+
 def body(snapshots):
     rows = snapshots.shape[0] // PAIRS
-    sharers = lax.axis_size(SUM_AXES)
+    sharers = lax.axis_size(PLANE_AXES)
     x = lax.all_to_all(snapshots, PAIR_AXES, 0, 0, tiled=True).reshape(PAIRS, rows, WIDE)
     keep, send = local_gram(x)
-    got = lax.ppermute(send, "c", [(0, 1), (1, 0)])
-    part = (keep + got).reshape(sharers, 1, -1)
-    part = jnp.sum(lax.all_to_all(part, SUM_AXES, 0, 0, tiled=True), axis=0, keepdims=True)
-    part = jnp.broadcast_to(part, (sharers, 1, part.shape[2]))
-    mine = lax.all_to_all(part, SUM_AXES, 0, 0, tiled=True).reshape(SHARE, WIDE, WIDE)
-    other = lax.ppermute(mine, "c", [(0, 1), (1, 0)])
+    part = (keep + swapped(send, "c", 1)).reshape(sharers, -1, WIDE)
+    part = jnp.sum(lax.all_to_all(part, PLANE_AXES, 0, 0, tiled=True), axis=0)
+    for by in (1, 2, 7):
+        part = part + swapped(part, "z", by)
+    part = jnp.broadcast_to(part[None], (sharers,) + part.shape)
+    mine = lax.all_to_all(part, PLANE_AXES, 0, 0, tiled=True).reshape(SHARE, WIDE, WIDE)
+    other = swapped(mine, "c", 1)
     y, norms = chain(mine, other, x)
     out = lax.all_to_all(y.reshape(snapshots.shape), PAIR_AXES, 0, 0, tiled=True)
     return out, norms.reshape(WIDE)

time: 216 us -> 191 us (0.88)
  blocking collectives: 146 us -> 103 us
  starting transfers between devices: 6.39 us -> 18.7 us
  waiting for transfers between devices: 5.16 us -> 10.9 us
    all_to_all x2, blocking collectives: 81.1 us -> 38 us  [the longest x1 21 us: body(): part = jnp.sum(lax.all_to_all(part, PLANE_AXES, 0, 0, tiled=True), axis=0)]
    ppermute x2 -> x5, starting transfers between devices: 6.39 us -> 18.7 us  [swapped(): lax.ppermute(x, axis, [(i, i ^ by) for i in range(lax.axis_size(axis))])]
    ppermute x2 -> x5, waiting for transfers between devices: 5.16 us -> 10.9 us  [swapped(): lax.ppermute(x, axis, [(i, i ^ by) for i in range(lax.axis_size(axis))])]
  transfers between devices with their start and end apart: 2 -> 5, of which waited for: 2 -> 5; matrix products, arithmetic and copies ran while one was open for 0% -> 0% of each run, Pallas kernels for 0% -> 0%
where the time goes in v3:
time: 191 us; the launch traced here: 190 us
  blocking collectives  103 us (54%)
  Pallas kernels  52.8 us (28%)
  starting transfers between devices  18.7 us (10%)
  waiting for transfers between devices  10.9 us (6%)
  local copies, waits for them, and re-layouts  2.42 us (1%)
    pallas_call x1, Pallas kernels, chain(): pl.pallas_call(chain_kernel, out_shape=(jax.ShapeDtypeStruct((PAIRS, rows...  47.1 us
    all_to_all x1, blocking collectives, body(): lax.all_to_all(snapshots, PAIR_AXES, 0, 0, tiled=True)  34.2 us
    all_to_all x1, blocking collectives, body(): lax.all_to_all(y.reshape(snapshots.shape), PAIR_AXES, 0, 0, tiled=True)  31.2 us
    all_to_all x1, blocking collectives, body(): part = jnp.sum(lax.all_to_all(part, PLANE_AXES, 0, 0, tiled=True), axis=0)  21 us
    ppermute x5, starting transfers between devices, swapped(): lax.ppermute(x, axis, [(i, i ^ by) for i in range(lax.axis_size(axis))])  18.7 us
    all_to_all x1, blocking collectives, body(): lax.all_to_all(part, PLANE_AXES, 0, 0, tiled=True)  17 us
    ppermute x5, waiting for transfers between devices, swapped(): lax.ppermute(x, axis, [(i, i ^ by) for i in range(lax.axis_size(axis))])  10.9 us
    pallas_call x1, Pallas kernels, local_gram(): pl.pallas_call(gram_kernel, out_shape=(out, out), scratch_shapes=[pltpu.V...  5.7 us
  transfers between devices with their start and end apart: 5, of which 5 were waited for; matrix products, arithmetic and copies ran while one was open for 0% of the time, Pallas kernels for 0%

profile of v3, /device:TPU:1, one launch (start us, length us, event | category | flops | bytes accessed | tf_op | source)
XLA Modules:
  0.0 190.3 jit_solution(6341725308255885157)
XLA Ops:
  0.6 34.2 %all_to_all.28.x_ref = f32[8,512,128]{2,1,0:T(8,128)} all-to-all(f32[8,512,128]{2,1,0:T(8,128)} %bitcast.9), channel_id=1, replica_groups=mesh['yl'=2,'z'=8,'c'=2,'x'=4,'yh'=2] {'x','yh'}, dimensions={0} | all-to-all | bytes 4194304 | tf_op jit(solution)/shard_map/all_to_all | solution.py:278
  34.8 5.7 %gram.1 = (f32[18,128,128]{2,1,0:T(8,128)}, f32[18,128,128]{2,1,0:T(8,128)}) custom-call(f32[8,512,128]{2,1,0:T(8,128)} %all_to_all.28.x_ref), custom_call_target="tpu_custom_call" | custom-call | tf_op jit(solution)/shard_map/gram/pallas_call | solution.py:233
  40.5 2.5 %collective-permute-start = (f32[18,128,128]{2,1,0:T(8,128)}, f32[18,128,128]{2,1,0:T(8,128)S(1)}, u32[]{:S(2)}, u32[]{:S(2)}) collective-permute-start(f32[18,128,128]{2,1,0:T(8,128)} %get-tuple-element.7), channel_id=1, source_target_pairs={{0,8},{8,0},{1,9},{9,1},{2,10},{10,2},{3,11},{11,3},{4,12},{12,4},... | collective-permute-start | bytes 3538952 | tf_op jit(solution)/shard_map/ppermute | solution.py:272
  43.0 2.7 %collective-permute-done = f32[18,128,128]{2,1,0:T(8,128)S(1)} collective-permute-done((f32[18,128,128]{2,1,0:T(8,128)}, f32[18,128,128]{2,1,0:T(8,128)S(1)}, u32[]{:S(2)}, u32[]{:S(2)}) %collective-permute-start) | collective-permute-done | bytes 1179680 | tf_op jit(solution)/shard_map/ppermute | solution.py:272
  45.7 1.4 add.12
  47.1 21.0 %all_to_all.29 = f32[16,144,128]{2,1,0:T(8,128)S(1)} all-to-all(f32[16,144,128]{2,1,0:T(8,128)S(1)} %bitcast.6), channel_id=1, replica_groups=mesh['yl'=2,'z'=8,'c'=2,'x'=4,'yh'=2] {'yl','x','yh'}, dimensions={0} | all-to-all | bytes 2359296 | tf_op jit(solution)/shard_map/all_to_all | solution.py:281
  68.1 0.1 reduce_sum.9
  68.2 1.7 collective-permute-start.1
  69.9 1.7 collective-permute-done.1
  71.7 3.1 %collective-permute-start.2 = (f32[144,128]{1,0:T(8,128)S(1)}, f32[144,128]{1,0:T(8,128)S(1)}, u32[]{:S(2)}, u32[]{:S(2)}) collective-permute-start(f32[144,128]{1,0:T(8,128)S(1)} %add.13), channel_id=1, source_target_pairs={{0,32},{16,48},{32,0},{48,16},{64,96},{80,112},{96,64},{112,80},{1... | collective-permute-start | bytes 221192 | tf_op jit(solution)/shard_map/ppermute | solution.py:272
  74.7 1.7 collective-permute-done.2
  76.5 5.6 %collective-permute-start.3 = (f32[144,128]{1,0:T(8,128)S(1)}, f32[144,128]{1,0:T(8,128)S(1)}, u32[]{:S(2)}, u32[]{:S(2)}) collective-permute-start(f32[144,128]{1,0:T(8,128)S(1)} %add.14), channel_id=1, source_target_pairs={{0,112},{16,96},{32,80},{48,64},{64,48},{80,32},{96,16},{112,0},{1... | collective-permute-start | bytes 221192 | tf_op jit(solution)/shard_map/ppermute | solution.py:272
  82.1 2.3 %collective-permute-done.3 = f32[144,128]{1,0:T(8,128)S(1)} collective-permute-done((f32[144,128]{1,0:T(8,128)S(1)}, f32[144,128]{1,0:T(8,128)S(1)}, u32[]{:S(2)}, u32[]{:S(2)}) %collective-permute-start.3) | collective-permute-done | bytes 73760 | tf_op jit(solution)/shard_map/ppermute | solution.py:272
  84.4 0.1 broadcast_in_dim.2
  84.5 17.0 %all_to_all.30 = f32[16,144,128]{2,1,0:T(8,128)S(1)} all-to-all(f32[16,144,128]{2,1,0:T(8,128)S(1)} %broadcast_in_dim.2), channel_id=1, replica_groups=mesh['yl'=2,'z'=8,'c'=2,'x'=4,'yh'=2] {'yl','x','yh'}, dimensions={0} | all-to-all | bytes 2359296 | tf_op jit(solution)/shard_map/all_to_all | solution.py:285
  101.5 0.0 copy-start
  101.5 5.7 %collective-permute-start.4 = (f32[18,128,128]{2,1,0:T(8,128)S(1)}, f32[18,128,128]{2,1,0:T(8,128)S(1)}, u32[]{:S(2)}, u32[]{:S(2)}) collective-permute-start(f32[18,128,128]{2,1,0:T(8,128)S(1)} %bitcast.7), channel_id=1, source_target_pairs={{0,8},{8,0},{1,9},{9,1},{2,10},{10,2},{3,11},{11,3},{4,12},{12,4},... | collective-permute-start | bytes 3538952 | tf_op jit(solution)/shard_map/ppermute | solution.py:272
  107.2 2.5 %collective-permute-done.4.other_ref = f32[18,128,128]{2,1,0:T(8,128)S(1)} collective-permute-done((f32[18,128,128]{2,1,0:T(8,128)S(1)}, f32[18,128,128]{2,1,0:T(8,128)S(1)}, u32[]{:S(2)}, u32[]{:S(2)}) %collective-permute-start.4) | collective-permute-done | bytes 1179680 | tf_op jit(solution)/shard_map/ppermute | solution.py:272
  109.7 0.0 copy-done
  109.7 0.0 copy-start.1
  109.7 1.0 copy-done.1
  110.7 47.1 %chain.1 = (f32[8,512,128]{2,1,0:T(8,128)}, f32[1,128]{1,0:T(1,128)}) custom-call(f32[18,128,128]{2,1,0:T(8,128)} %bitcast.8, f32[18,128,128]{2,1,0:T(8,128)} %copy-done.1, f32[8,512,128]{2,1,0:T(8,128)} %all_to_all.28.x_ref), custom_call_target="tpu_custom_call" | custom-call | tf_op jit(solution)/shard_map/chain/pallas_call | solution.py:248
  157.8 31.2 %all_to_all.31 = f32[8,512,128]{2,1,0:T(8,128)S(1)} all-to-all(f32[8,512,128]{2,1,0:T(8,128)} %get-tuple-element.8), channel_id=1, replica_groups=mesh['yl'=2,'z'=8,'c'=2,'x'=4,'yh'=2] {'x','yh'}, dimensions={0} | all-to-all | bytes 4194304 | tf_op jit(solution)/shard_map/all_to_all | solution.py:288
  189.0 1.3 copy.4
  (3 shorter events, 0.0 us)
Async XLA Ops:
  40.5 5.2 %collective-permute-start = (f32[18,128,128]{2,1,0:T(8,128)}, f32[18,128,128]{2,1,0:T(8,128)S(1)}, u32[]{:S(2)}, u32[]{:S(2)}) collective-permute-start(f32[18,128,128]{2,1,0:T(8,128)} %get-tuple-element.7), channel_id=1, source_target_pairs={{0,8},{8,0},{1,9},{9,1},{2,10},{10,2},{3,11},{11,3},{4,12},{12,4},... | collective-permute-start | bytes 3538952 | tf_op jit(solution)/shard_map/ppermute | solution.py:272
  68.2 3.5 %collective-permute-start.1 = (f32[144,128]{1,0:T(8,128)S(1)}, f32[144,128]{1,0:T(8,128)S(1)}, u32[]{:S(2)}, u32[]{:S(2)}) collective-permute-start(f32[144,128]{1,0:T(8,128)S(1)} %reduce_sum.9), channel_id=1, source_target_pairs={{0,16},{16,0},{32,48},{48,32},{64,80},{80,64},{96,112},{112,96},{1... | collective-permute-start | bytes 221192 | tf_op jit(solution)/shard_map/ppermute | solution.py:272
  71.7 4.8 %collective-permute-start.2 = (f32[144,128]{1,0:T(8,128)S(1)}, f32[144,128]{1,0:T(8,128)S(1)}, u32[]{:S(2)}, u32[]{:S(2)}) collective-permute-start(f32[144,128]{1,0:T(8,128)S(1)} %add.13), channel_id=1, source_target_pairs={{0,32},{16,48},{32,0},{48,16},{64,96},{80,112},{96,64},{112,80},{1... | collective-permute-start | bytes 221192 | tf_op jit(solution)/shard_map/ppermute | solution.py:272
  76.5 7.9 %collective-permute-start.3 = (f32[144,128]{1,0:T(8,128)S(1)}, f32[144,128]{1,0:T(8,128)S(1)}, u32[]{:S(2)}, u32[]{:S(2)}) collective-permute-start(f32[144,128]{1,0:T(8,128)S(1)} %add.14), channel_id=1, source_target_pairs={{0,112},{16,96},{32,80},{48,64},{64,48},{80,32},{96,16},{112,0},{1... | collective-permute-start | bytes 221192 | tf_op jit(solution)/shard_map/ppermute | solution.py:272
  101.5 8.2 %copy-start = (f32[16,144,128]{2,1,0:T(8,128)}, f32[16,144,128]{2,1,0:T(8,128)S(1)}, u32[]{:S(2)}) copy-start(f32[16,144,128]{2,1,0:T(8,128)S(1)} %all_to_all.30) | copy-start | bytes 3538948
  101.5 8.2 %collective-permute-start.4 = (f32[18,128,128]{2,1,0:T(8,128)S(1)}, f32[18,128,128]{2,1,0:T(8,128)S(1)}, u32[]{:S(2)}, u32[]{:S(2)}) collective-permute-start(f32[18,128,128]{2,1,0:T(8,128)S(1)} %bitcast.7), channel_id=1, source_target_pairs={{0,8},{8,0},{1,9},{9,1},{2,10},{10,2},{3,11},{11,3},{4,12},{12,4},... | collective-permute-start | bytes 3538952 | tf_op jit(solution)/shard_map/ppermute | solution.py:272
  109.7 1.0 copy-start.1

commit v4 on v3

v4 whole, which is shorter than its diff:
```python
import jax
import jax.numpy as jnp
from jax import lax
from jax.experimental import pallas as pl
from jax.experimental.pallas import tpu as pltpu
from jax.sharding import PartitionSpec as P

STEPS = 6
HALF = 64
WIDE = 2 * HALF
PAIRS = 8
BLOCKS = [(i, j) for i in range(PAIRS) for j in range(i, PAIRS)]
INDEX = {block: t for t, block in enumerate(BLOCKS)}
SHARE = len(BLOCKS) // 2

PAIR_AXES = ("x", "yh")
PLANE_AXES = ("yl", "x", "yh")
F32 = jnp.float32
BF16 = jnp.bfloat16
MIB = 1024 * 1024
DOUBLINGS = 4

MOVED = {0: 0, 1: 2, 2 * PAIRS - 2: 2 * PAIRS - 1}
for place in range(1, PAIRS - 1):
    MOVED[2 * place] = 2 * (place + 1)
for place in range(1, PAIRS):
    MOVED[2 * place + 1] = 2 * (place - 1) + 1


def sources(block):
    return [next(t for t, u in MOVED.items() if u == b) for b in block]


def updates():
    lists = []
    needed = {(2 * k + a, 2 * k + b) for k in range(PAIRS) for a in range(2) for b in range(a, 2)}
    inside = set(needed)
    for _ in range(STEPS - 1):
        blocks = set()
        for block in needed:
            old = sorted(sources(block))
            blocks.add((old[0] // 2, old[1] // 2))
        lists.insert(0, sorted(blocks))
        needed = set(inside)
        for i, j in blocks:
            needed |= {tuple(sorted((2 * i + a, 2 * j + b))) for a in range(2) for b in range(2)}
    return lists


def split(x):
    high = x.astype(BF16)
    low = (x - high.astype(F32)).astype(BF16)
    return high, low


def beside(x):
    return jnp.concatenate(split(x), axis=1)


def twice(both):
    return jnp.concatenate([both, both], axis=0)


def mul(a, b):
    y = jnp.dot(a, b, preferred_element_type=F32)
    n = y.shape[1] // 2
    return y[:, :n] + y[:, n:]


def gram_kernel(x_ref, keep_ref, send_ref, lhs, rhs):
    core = lax.axis_index("c")
    for k in range(PAIRS):
        x = x_ref[k]
        rhs[k] = jnp.concatenate(split(x), axis=1)
        lhs[k] = jnp.concatenate(split(x.T), axis=0)

    def block(i, j):
        y = jnp.dot(lhs[i], rhs[j], preferred_element_type=F32)
        y = y[:WIDE] + y[WIDE:]
        return y[:, :WIDE] + y[:, WIDE:]

    for t in range(SHARE):
        first = block(*BLOCKS[t])
        second = block(*BLOCKS[t + SHARE])
        keep_ref[t] = jnp.where(core == 0, first, second)
        send_ref[t] = jnp.where(core == 0, second, first)


def chain_kernel(mine_ref, other_ref, x_ref, y_ref, norms_ref, gram, half, data, after, skew, inv, turn, turned, norms):
    core = lax.axis_index("c")
    position = lax.axis_index("x") * 2 + lax.axis_index("yh")
    row = lax.broadcasted_iota(jnp.int32, (WIDE, WIDE), 0)
    col = lax.broadcasted_iota(jnp.int32, (WIDE, WIDE), 1)
    eye = (row == col).astype(F32)
    for t in range(len(BLOCKS)):
        gram[t] = jnp.where(core == t // SHARE, mine_ref[t % SHARE], other_ref[t % SHARE])
    for k in range(PAIRS):
        data[k] = beside(x_ref[k])

    def correct(k):
        p = inv[k]
        e = eye - p + mul(beside(skew[k]), twice(beside(p)))
        inv[k] = p + jnp.dot(p.astype(BF16), e.astype(BF16), preferred_element_type=F32)
        return jnp.sum(e * e, axis=(0, 1), keepdims=True)

    def correct_all():
        worst = jnp.zeros((1, 1), F32)
        for k in range(PAIRS):
            worst = jnp.maximum(worst, correct(k))
        return worst[0, 0]

    def rotations():
        powers, rates = [], []
        for k in range(PAIRS):
            g = gram[INDEX[k, k]]
            diag = g * eye
            total = jnp.sum(diag, axis=0, keepdims=True) + jnp.sum(diag, axis=1, keepdims=True)
            ratio = jnp.clip(0.5 * (g / total), -0.25, 0.25)
            s = jnp.where(col > row, ratio, jnp.where(col < row, -ratio, 0.0))
            skew[k] = s
            both = beside(s)
            square = mul(both, twice(both))
            bound = jnp.sqrt(0.5 * jnp.sum(square * square, axis=(0, 1), keepdims=True)) * 1.001
            scale = 2.0 / (2.0 + bound)
            powers.append((1.0 - scale) * eye + scale * square)
            inv[k] = scale * (eye + s)
            rates.append(bound / (2.0 + bound))
        for time in range(DOUBLINGS):
            last = time == DOUBLINGS - 1
            for k in range(PAIRS):
                p = inv[k]
                both = beside(powers[k])
                stack = beside(p) if last else jnp.concatenate([beside(p), both], axis=0)
                y = mul(stack, twice(both))
                rate = rates[k] * rates[k] / (2.0 - rates[k] * rates[k])
                inv[k] = (1.0 + rate) * (p + y[:WIDE])
                if not last:
                    powers[k] = (1.0 + rate) * y[WIDE:] - rate * eye
                rates[k] = rate
        lax.while_loop(
            lambda c: jnp.logical_and(c[1] > 3e-5, c[0] < 40),
            lambda c: (c[0] + 1, correct_all()),
            (0, correct_all()),
        )
        for k in range(PAIRS):
            j = 2.0 * inv[k] - eye
            turn[k] = twice(beside(j))
            turned[k] = beside(j.T)

    def put(ref, lead, value, a, b, to_a, to_b):
        part = value[a * HALF : (a + 1) * HALF, :]
        if b != to_b:
            part = pltpu.roll(part, HALF, 1)
        ref[lead, pl.ds(to_a * HALF, HALF), pl.ds(to_b * HALF, HALF)] = part[:, to_b * HALF : (to_b + 1) * HALF]

    def rotate_gram(blocks):
        for i, j in blocks:
            half[INDEX[i, j]] = beside(mul(beside(gram[INDEX[i, j]]), turn[j]))
        for i, j in blocks:
            g = mul(turned[i], twice(half[INDEX[i, j]]))
            flipped = None
            for a in range(2):
                for b in range(2):
                    to_i, to_j = MOVED[2 * i + a], MOVED[2 * j + b]
                    if i == j and a != b and to_i > to_j:
                        continue
                    low, high = min(to_i, to_j), max(to_i, to_j)
                    target = INDEX[low // 2, high // 2]
                    within = low // 2 == high // 2 and low != high
                    if to_i <= to_j or within:
                        put(gram, target, g, a, b, to_i % 2, to_j % 2)
                    if to_i > to_j or within:
                        flipped = g.T if flipped is None else flipped
                        put(gram, target, flipped, b, a, to_j % 2, to_i % 2)

    def halves(k, value):
        for b in range(2):
            to = MOVED[2 * k + b]
            yield to // 2, to % 2 * HALF, value if b == to % 2 else pltpu.roll(value, HALF, 1)

    def rotate_data(now, later):
        for k in range(PAIRS):
            for to, side, part in halves(k, mul(now[k], turn[k])):
                high, low = split(part)
                later[to, :, pl.ds(side, HALF)] = high[:, side : side + HALF]
                later[to, :, pl.ds(WIDE + side, HALF)] = low[:, side : side + HALF]

    lists = updates() + [[]]

    def two_steps(trip, carry):
        for odd in range(2):
            rotations()
            for t in range(STEPS // 2):

                @pl.when(trip == t)
                def _():
                    rotate_gram(lists[2 * t + odd])

            if odd == 0:
                rotate_data(data, after)
            else:

                @pl.when(trip < STEPS // 2 - 1)
                def _():
                    rotate_data(after, data)

        return carry

    lax.fori_loop(0, STEPS // 2, two_steps, 0)
    for k in range(PAIRS):
        for to, side, part in halves(k, mul(after[k], turn[k])):
            y_ref[to, :, pl.ds(side, HALF)] = part[:, side : side + HALF]
    for k in range(PAIRS):
        j = 2.0 * inv[k] - eye
        h = mul(beside(gram[INDEX[k, k]]), turn[k])
        n = jnp.sqrt(jnp.maximum(jnp.sum(j * h, axis=0, keepdims=True), 0.0))
        for to, side, part in halves(k, n):
            norms[to, :, pl.ds(side, HALF)] = part[:, side : side + HALF]
    norms_ref[...] = norms[position]


def local_gram(x):
    rows = x.shape[1]
    out = jax.ShapeDtypeStruct((SHARE, WIDE, WIDE), F32)
    return pl.pallas_call(
        gram_kernel,
        out_shape=(out, out),
        scratch_shapes=[
            pltpu.VMEM((PAIRS, 2 * WIDE, rows), BF16),
            pltpu.VMEM((PAIRS, rows, 2 * WIDE), BF16),
        ],
        compiler_params=pltpu.CompilerParams(vmem_limit_bytes=16 * MIB),
        name="gram",
    )(x)


def chain(mine, other, x):
    rows = x.shape[1]
    square = pltpu.VMEM((PAIRS, WIDE, WIDE), F32)
    return pl.pallas_call(
        chain_kernel,
        out_shape=(
            jax.ShapeDtypeStruct((PAIRS, rows, WIDE), F32),
            jax.ShapeDtypeStruct((1, WIDE), F32),
        ),
        scratch_shapes=[
            pltpu.VMEM((len(BLOCKS), WIDE, WIDE), F32),
            pltpu.VMEM((len(BLOCKS), WIDE, 2 * WIDE), BF16),
            pltpu.VMEM((PAIRS, rows, 2 * WIDE), BF16),
            pltpu.VMEM((PAIRS, rows, 2 * WIDE), BF16),
            square,
            square,
            pltpu.VMEM((PAIRS, 2 * WIDE, 2 * WIDE), BF16),
            pltpu.VMEM((PAIRS, WIDE, 2 * WIDE), BF16),
            pltpu.VMEM((PAIRS, 1, WIDE), F32),
        ],
        compiler_params=pltpu.CompilerParams(vmem_limit_bytes=32 * MIB),
        name="chain",
    )(mine, other, x)


def swapped(x, axis, by):
    return lax.ppermute(x, axis, [(i, i ^ by) for i in range(lax.axis_size(axis))])


def body(snapshots):
    rows = snapshots.shape[0] // PAIRS
    sharers = lax.axis_size(PLANE_AXES)
    x = lax.all_to_all(snapshots, PAIR_AXES, 0, 0, tiled=True).reshape(PAIRS, rows, WIDE)
    keep, send = local_gram(x)
    part = (keep + swapped(send, "c", 1)).reshape(sharers, -1, WIDE)
    part = jnp.sum(lax.all_to_all(part, PLANE_AXES, 0, 0, tiled=True), axis=0)
    for by in (1, 2, 7):
        part = part + swapped(part, "z", by)
    part = jnp.broadcast_to(part[None], (sharers,) + part.shape)
    mine = lax.all_to_all(part, PLANE_AXES, 0, 0, tiled=True).reshape(SHARE, WIDE, WIDE)
    other = swapped(mine, "c", 1)
    y, norms = chain(mine, other, x)
    out = lax.all_to_all(y.reshape(snapshots.shape), PAIR_AXES, 0, 0, tiled=True)
    return out, norms.reshape(WIDE)


def solution(mesh):
    axes = ("yl", "z", "c", "x", "yh")
    finer = jax.sharding.Mesh(mesh.devices.reshape(2, 8, 2, 4, 2), axes)
    rows, pairs = ("yl", "z", "c"), PAIR_AXES
    return jax.shard_map(
        body,
        mesh=finer,
        in_specs=(P(rows, pairs),),
        out_specs=(P(rows, pairs), P(pairs)),
        check_vma=False,
    )
```

time: 191 us -> 174 us (0.911)
  Pallas kernels: 52.8 us -> 40.2 us
    pallas_call x1, Pallas kernels: 47.1 us -> 37.5 us  [chain(): pl.pallas_call(chain_kernel, out_shape=(jax.ShapeDtypeStruct((PAIRS, rows...]
    pallas_call x1, Pallas kernels: 5.7 us -> 2.7 us  [local_gram(): pl.pallas_call(gram_kernel, out_shape=(out, out), scratch_shapes=[pltpu.V...]
where the time goes in v4:
time: 174 us
  blocking collectives  102 us (59%)
  Pallas kernels  40.2 us (23%)
  starting transfers between devices  18.7 us (11%)
  waiting for transfers between devices  10.7 us (6%)
    pallas_call x1, Pallas kernels, chain(): pl.pallas_call(chain_kernel, out_shape=(jax.ShapeDtypeStruct((PAIRS, rows...  37.5 us
    all_to_all x1, blocking collectives, body(): lax.all_to_all(snapshots, PAIR_AXES, 0, 0, tiled=True)  34.1 us
    all_to_all x1, blocking collectives, body(): lax.all_to_all(y.reshape(snapshots.shape), PAIR_AXES, 0, 0, tiled=True)  29.9 us
    all_to_all x1, blocking collectives, body(): part = jnp.sum(lax.all_to_all(part, PLANE_AXES, 0, 0, tiled=True), axis=0)  21 us
    ppermute x5, starting transfers between devices, swapped(): lax.ppermute(x, axis, [(i, i ^ by) for i in range(lax.axis_size(axis))])  18.7 us
    all_to_all x1, blocking collectives, body(): lax.all_to_all(part, PLANE_AXES, 0, 0, tiled=True)  17 us
    ppermute x5, waiting for transfers between devices, swapped(): lax.ppermute(x, axis, [(i, i ^ by) for i in range(lax.axis_size(axis))])  10.7 us
  transfers between devices with their start and end apart: 5, of which 5 were waited for; matrix products, arithmetic and copies ran while one was open for 0% of the time, Pallas kernels for 0%

profile of v4, /device:TPU:1, one launch (start us, length us, event | category | flops | bytes accessed | tf_op | source)
XLA Modules:
  0.0 173.9 jit_solution(6780670312066217517)
XLA Ops:
  0.6 34.1 %all_to_all.28.x_ref = f32[8,512,128]{2,1,0:T(8,128)S(1)} all-to-all(f32[8,512,128]{2,1,0:T(8,128)} %bitcast.9), channel_id=1, replica_groups=mesh['yl'=2,'z'=8,'c'=2,'x'=4,'yh'=2] {'x','yh'}, dimensions={0} | all-to-all | bytes 4194304 | tf_op jit(solution)/shard_map/all_to_all | solution.py:269
  34.7 2.7 %gram.1 = (f32[18,128,128]{2,1,0:T(8,128)S(1)}, f32[18,128,128]{2,1,0:T(8,128)S(1)}) custom-call(f32[8,512,128]{2,1,0:T(8,128)S(1)} %all_to_all.28.x_ref), custom_call_target="tpu_custom_call" | custom-call | tf_op jit(solution)/shard_map/gram/pallas_call | solution.py:225
  37.4 2.6 %collective-permute-start = (f32[18,128,128]{2,1,0:T(8,128)S(1)}, f32[18,128,128]{2,1,0:T(8,128)S(1)}, u32[]{:S(2)}, u32[]{:S(2)}) collective-permute-start(f32[18,128,128]{2,1,0:T(8,128)S(1)} %get-tuple-element.7), channel_id=1, source_target_pairs={{0,8},{8,0},{1,9},{9,1},{2,10},{10,2},{3,11},{11,3},{4,12},{12,4},... | collective-permute-start | bytes 3538952 | tf_op jit(solution)/shard_map/ppermute | solution.py:263
  40.0 2.5 %collective-permute-done = f32[18,128,128]{2,1,0:T(8,128)S(1)} collective-permute-done((f32[18,128,128]{2,1,0:T(8,128)S(1)}, f32[18,128,128]{2,1,0:T(8,128)S(1)}, u32[]{:S(2)}, u32[]{:S(2)}) %collective-permute-start) | collective-permute-done | bytes 1179680 | tf_op jit(solution)/shard_map/ppermute | solution.py:263
  42.4 0.1 add.12
  42.6 21.0 %all_to_all.29 = f32[16,144,128]{2,1,0:T(8,128)S(1)} all-to-all(f32[16,144,128]{2,1,0:T(8,128)S(1)} %bitcast.8), channel_id=1, replica_groups=mesh['yl'=2,'z'=8,'c'=2,'x'=4,'yh'=2] {'yl','x','yh'}, dimensions={0} | all-to-all | bytes 2359296 | tf_op jit(solution)/shard_map/all_to_all | solution.py:272
  63.6 0.1 reduce_sum.9
  63.7 1.7 collective-permute-start.1
  65.4 1.7 %collective-permute-done.1 = f32[144,128]{1,0:T(8,128)S(1)} collective-permute-done((f32[144,128]{1,0:T(8,128)S(1)}, f32[144,128]{1,0:T(8,128)S(1)}, u32[]{:S(2)}, u32[]{:S(2)}) %collective-permute-start.1) | collective-permute-done | bytes 73760 | tf_op jit(solution)/shard_map/ppermute | solution.py:263
  67.2 3.1 %collective-permute-start.2 = (f32[144,128]{1,0:T(8,128)S(1)}, f32[144,128]{1,0:T(8,128)S(1)}, u32[]{:S(2)}, u32[]{:S(2)}) collective-permute-start(f32[144,128]{1,0:T(8,128)S(1)} %add.13), channel_id=1, source_target_pairs={{0,32},{16,48},{32,0},{48,16},{64,96},{80,112},{96,64},{112,80},{1... | collective-permute-start | bytes 221192 | tf_op jit(solution)/shard_map/ppermute | solution.py:263
  70.2 1.7 %collective-permute-done.2 = f32[144,128]{1,0:T(8,128)S(1)} collective-permute-done((f32[144,128]{1,0:T(8,128)S(1)}, f32[144,128]{1,0:T(8,128)S(1)}, u32[]{:S(2)}, u32[]{:S(2)}) %collective-permute-start.2) | collective-permute-done | bytes 73760 | tf_op jit(solution)/shard_map/ppermute | solution.py:263
  72.0 5.6 %collective-permute-start.3 = (f32[144,128]{1,0:T(8,128)S(1)}, f32[144,128]{1,0:T(8,128)S(1)}, u32[]{:S(2)}, u32[]{:S(2)}) collective-permute-start(f32[144,128]{1,0:T(8,128)S(1)} %add.14), channel_id=1, source_target_pairs={{0,112},{16,96},{32,80},{48,64},{64,48},{80,32},{96,16},{112,0},{1... | collective-permute-start | bytes 221192 | tf_op jit(solution)/shard_map/ppermute | solution.py:263
  77.6 2.3 %collective-permute-done.3 = f32[144,128]{1,0:T(8,128)S(1)} collective-permute-done((f32[144,128]{1,0:T(8,128)S(1)}, f32[144,128]{1,0:T(8,128)S(1)}, u32[]{:S(2)}, u32[]{:S(2)}) %collective-permute-start.3) | collective-permute-done | bytes 73760 | tf_op jit(solution)/shard_map/ppermute | solution.py:263
  79.9 0.1 broadcast_in_dim.2
  80.0 17.0 %all_to_all.30 = f32[16,144,128]{2,1,0:T(8,128)S(1)} all-to-all(f32[16,144,128]{2,1,0:T(8,128)S(1)} %broadcast_in_dim.2), channel_id=1, replica_groups=mesh['yl'=2,'z'=8,'c'=2,'x'=4,'yh'=2] {'yl','x','yh'}, dimensions={0} | all-to-all | bytes 2359296 | tf_op jit(solution)/shard_map/all_to_all | solution.py:276
  97.0 5.7 %collective-permute-start.4 = (f32[18,128,128]{2,1,0:T(8,128)S(1)}, f32[18,128,128]{2,1,0:T(8,128)S(1)}, u32[]{:S(2)}, u32[]{:S(2)}) collective-permute-start(f32[18,128,128]{2,1,0:T(8,128)S(1)} %bitcast.5), channel_id=1, source_target_pairs={{0,8},{8,0},{1,9},{9,1},{2,10},{10,2},{3,11},{11,3},{4,12},{12,4},... | collective-permute-start | bytes 3538952 | tf_op jit(solution)/shard_map/ppermute | solution.py:263
  102.7 2.5 %collective-permute-done.4.other_ref = f32[18,128,128]{2,1,0:T(8,128)S(1)} collective-permute-done((f32[18,128,128]{2,1,0:T(8,128)S(1)}, f32[18,128,128]{2,1,0:T(8,128)S(1)}, u32[]{:S(2)}, u32[]{:S(2)}) %collective-permute-start.4) | collective-permute-done | bytes 1179680 | tf_op jit(solution)/shard_map/ppermute | solution.py:263
  105.2 37.5 %chain.1 = (f32[8,512,128]{2,1,0:T(8,128)S(1)}, f32[1,128]{1,0:T(1,128)}) custom-call(f32[18,128,128]{2,1,0:T(8,128)S(1)} %bitcast.6, f32[18,128,128]{2,1,0:T(8,128)S(1)} %collective-permute-done.4.other_ref, f32[8,512,128]{2,1,0:T(8,128)S(1)} %all_to_all.28.x_ref), custom_call_target="tpu_custom_call" | custom-call | tf_op jit(solution)/shard_map/chain/pallas_call | solution.py:240
  142.7 29.9 %all_to_all.31 = f32[8,512,128]{2,1,0:T(8,128)S(1)} all-to-all(f32[8,512,128]{2,1,0:T(8,128)S(1)} %get-tuple-element.8), channel_id=1, replica_groups=mesh['yl'=2,'z'=8,'c'=2,'x'=4,'yh'=2] {'x','yh'}, dimensions={0} | all-to-all | bytes 4194304 | tf_op jit(solution)/shard_map/all_to_all | solution.py:279
  172.6 1.3 copy.4
  (3 shorter events, 0.0 us)
Async XLA Ops:
  37.4 5.0 %collective-permute-start = (f32[18,128,128]{2,1,0:T(8,128)S(1)}, f32[18,128,128]{2,1,0:T(8,128)S(1)}, u32[]{:S(2)}, u32[]{:S(2)}) collective-permute-start(f32[18,128,128]{2,1,0:T(8,128)S(1)} %get-tuple-element.7), channel_id=1, source_target_pairs={{0,8},{8,0},{1,9},{9,1},{2,10},{10,2},{3,11},{11,3},{4,12},{12,4},... | collective-permute-start | bytes 3538952 | tf_op jit(solution)/shard_map/ppermute | solution.py:263
  63.7 3.5 %collective-permute-start.1 = (f32[144,128]{1,0:T(8,128)S(1)}, f32[144,128]{1,0:T(8,128)S(1)}, u32[]{:S(2)}, u32[]{:S(2)}) collective-permute-start(f32[144,128]{1,0:T(8,128)S(1)} %reduce_sum.9), channel_id=1, source_target_pairs={{0,16},{16,0},{32,48},{48,32},{64,80},{80,64},{96,112},{112,96},{1... | collective-permute-start | bytes 221192 | tf_op jit(solution)/shard_map/ppermute | solution.py:263
  67.2 4.8 %collective-permute-start.2 = (f32[144,128]{1,0:T(8,128)S(1)}, f32[144,128]{1,0:T(8,128)S(1)}, u32[]{:S(2)}, u32[]{:S(2)}) collective-permute-start(f32[144,128]{1,0:T(8,128)S(1)} %add.13), channel_id=1, source_target_pairs={{0,32},{16,48},{32,0},{48,16},{64,96},{80,112},{96,64},{112,80},{1... | collective-permute-start | bytes 221192 | tf_op jit(solution)/shard_map/ppermute | solution.py:263
  72.0 7.9 %collective-permute-start.3 = (f32[144,128]{1,0:T(8,128)S(1)}, f32[144,128]{1,0:T(8,128)S(1)}, u32[]{:S(2)}, u32[]{:S(2)}) collective-permute-start(f32[144,128]{1,0:T(8,128)S(1)} %add.14), channel_id=1, source_target_pairs={{0,112},{16,96},{32,80},{48,64},{64,48},{80,32},{96,16},{112,0},{1... | collective-permute-start | bytes 221192 | tf_op jit(solution)/shard_map/ppermute | solution.py:263
  97.0 8.2 %collective-permute-start.4 = (f32[18,128,128]{2,1,0:T(8,128)S(1)}, f32[18,128,128]{2,1,0:T(8,128)S(1)}, u32[]{:S(2)}, u32[]{:S(2)}) collective-permute-start(f32[18,128,128]{2,1,0:T(8,128)S(1)} %bitcast.5), channel_id=1, source_target_pairs={{0,8},{8,0},{1,9},{9,1},{2,10},{10,2},{3,11},{11,3},{4,12},{12,4},... | collective-permute-start | bytes 3538952 | tf_op jit(solution)/shard_map/ppermute | solution.py:263

commit v5 on v4

--- a/solution.py
+++ b/solution.py
@@ -19,6 +19,7 @@
 BF16 = jnp.bfloat16
 MIB = 1024 * 1024
 DOUBLINGS = 4
+GROUP = 4
 
 MOVED = {0: 0, 1: 2, 2 * PAIRS - 2: 2 * PAIRS - 1}
 for place in range(1, PAIRS - 1):
@@ -61,17 +62,23 @@
     return jnp.concatenate([both, both], axis=0)
 
 
+def three(x):
+    high, middle = split(x)
+    low = (x - high.astype(F32) - middle.astype(F32)).astype(BF16)
+    return jnp.concatenate([high, middle], axis=1), low
+
+
 def mul(a, b):
     y = jnp.dot(a, b, preferred_element_type=F32)
     n = y.shape[1] // 2
     return y[:, :n] + y[:, n:]
 
 
-def gram_kernel(x_ref, keep_ref, send_ref, lhs, rhs):
+def gram_kernel(x_ref, keep_ref, send_ref, rhs, lhs):
     core = lax.axis_index("c")
     for k in range(PAIRS):
         x = x_ref[k]
-        rhs[k] = jnp.concatenate(split(x), axis=1)
+        rhs[k] = beside(x)
         lhs[k] = jnp.concatenate(split(x.T), axis=0)
 
     def block(i, j):
@@ -86,7 +93,7 @@
         send_ref[t] = jnp.where(core == 0, second, first)
 
 
-def chain_kernel(mine_ref, other_ref, x_ref, y_ref, norms_ref, gram, half, data, after, skew, inv, turn, turned, norms):
+def chain_kernel(mine_ref, other_ref, x_ref, y_ref, norms_ref, gram, half, rest, data, after, skew, inv, turn, turned, norms):
     core = lax.axis_index("c")
     position = lax.axis_index("x") * 2 + lax.axis_index("yh")
     row = lax.broadcasted_iota(jnp.int32, (WIDE, WIDE), 0)
@@ -94,8 +101,6 @@
     eye = (row == col).astype(F32)
     for t in range(len(BLOCKS)):
         gram[t] = jnp.where(core == t // SHARE, mine_ref[t % SHARE], other_ref[t % SHARE])
-    for k in range(PAIRS):
-        data[k] = beside(x_ref[k])
 
     def correct(k):
         p = inv[k]
@@ -154,10 +159,19 @@
         ref[lead, pl.ds(to_a * HALF, HALF), pl.ds(to_b * HALF, HALF)] = part[:, to_b * HALF : (to_b + 1) * HALF]
 
     def rotate_gram(blocks):
+        for j in range(PAIRS):
+            column = [INDEX[block] for block in blocks if block[1] == j]
+            for start in range(0, len(column), GROUP):
+                group = column[start : start + GROUP]
+                parts = [three(gram[t]) for t in group]
+                h = mul(jnp.concatenate([both for both, _ in parts], axis=0), turn[j])
+                low = jnp.concatenate([low for _, low in parts], axis=0)
+                h = h + jnp.dot(low, turn[j, :WIDE, :WIDE], preferred_element_type=F32)
+                for place, t in enumerate(group):
+                    half[t], rest[t] = three(h[place * WIDE : (place + 1) * WIDE])
         for i, j in blocks:
-            half[INDEX[i, j]] = beside(mul(beside(gram[INDEX[i, j]]), turn[j]))
-        for i, j in blocks:
-            g = mul(turned[i], twice(half[INDEX[i, j]]))
+            t = INDEX[i, j]
+            g = mul(turned[i], twice(half[t])) + jnp.dot(turned[i, :, :WIDE], rest[t], preferred_element_type=F32)
             flipped = None
             for a in range(2):
                 for b in range(2):
@@ -197,7 +211,15 @@
                     rotate_gram(lists[2 * t + odd])
 
             if odd == 0:
-                rotate_data(data, after)
+
+                @pl.when(trip == 0)
+                def _():
+                    rotate_data(x_ref, after)
+
+                @pl.when(trip > 0)
+                def _():
+                    rotate_data(data, after)
+
             else:
 
                 @pl.when(trip < STEPS // 2 - 1)
@@ -224,10 +246,9 @@
     out = jax.ShapeDtypeStruct((SHARE, WIDE, WIDE), F32)
     return pl.pallas_call(
         gram_kernel,
-        out_shape=(out, out),
+        out_shape=(out, out, jax.ShapeDtypeStruct((PAIRS, rows, 2 * WIDE), BF16)),
         scratch_shapes=[
             pltpu.VMEM((PAIRS, 2 * WIDE, rows), BF16),
-            pltpu.VMEM((PAIRS, rows, 2 * WIDE), BF16),
         ],
         compiler_params=pltpu.CompilerParams(vmem_limit_bytes=16 * MIB),
         name="gram",
@@ -246,6 +267,7 @@
         scratch_shapes=[
             pltpu.VMEM((len(BLOCKS), WIDE, WIDE), F32),
             pltpu.VMEM((len(BLOCKS), WIDE, 2 * WIDE), BF16),
+            pltpu.VMEM((len(BLOCKS), WIDE, WIDE), BF16),
             pltpu.VMEM((PAIRS, rows, 2 * WIDE), BF16),
             pltpu.VMEM((PAIRS, rows, 2 * WIDE), BF16),
             square,
@@ -267,7 +289,7 @@
     rows = snapshots.shape[0] // PAIRS
     sharers = lax.axis_size(PLANE_AXES)
     x = lax.all_to_all(snapshots, PAIR_AXES, 0, 0, tiled=True).reshape(PAIRS, rows, WIDE)
-    keep, send = local_gram(x)
+    keep, send, x = local_gram(x)
     part = (keep + swapped(send, "c", 1)).reshape(sharers, -1, WIDE)
     part = jnp.sum(lax.all_to_all(part, PLANE_AXES, 0, 0, tiled=True), axis=0)
     for by in (1, 2, 7):

time: 174 us -> 175 us (level)
  no operation moved by 1% of the time
where the time goes in v5:
time: 175 us; the launch traced here: 173 us
  blocking collectives  102 us (58%)
  Pallas kernels  39.7 us (23%)
  starting transfers between devices  18.7 us (11%)
  waiting for transfers between devices  10.7 us (6%)
    pallas_call x1, Pallas kernels, chain(): pl.pallas_call(chain_kernel, out_shape=(jax.ShapeDtypeStruct((PAIRS, rows...  37 us
    all_to_all x1, blocking collectives, body(): lax.all_to_all(snapshots, PAIR_AXES, 0, 0, tiled=True)  34.1 us
    all_to_all x1, blocking collectives, body(): lax.all_to_all(y.reshape(snapshots.shape), PAIR_AXES, 0, 0, tiled=True)  29.9 us
    all_to_all x1, blocking collectives, body(): part = jnp.sum(lax.all_to_all(part, PLANE_AXES, 0, 0, tiled=True), axis=0)  21 us
    ppermute x5, starting transfers between devices, swapped(): lax.ppermute(x, axis, [(i, i ^ by) for i in range(lax.axis_size(axis))])  18.7 us
    all_to_all x1, blocking collectives, body(): lax.all_to_all(part, PLANE_AXES, 0, 0, tiled=True)  17 us
    ppermute x5, waiting for transfers between devices, swapped(): lax.ppermute(x, axis, [(i, i ^ by) for i in range(lax.axis_size(axis))])  10.7 us
  transfers between devices with their start and end apart: 5, of which 5 were waited for; matrix products, arithmetic and copies ran while one was open for 0% of the time, Pallas kernels for 0%

profile of v5, /device:TPU:1, one launch (start us, length us, event | category | flops | bytes accessed | tf_op | source)
XLA Modules:
  0.0 173.4 jit_solution(10705585891420917890)
XLA Ops:
  0.6 34.1 %all_to_all.28.x_ref = f32[8,512,128]{2,1,0:T(8,128)S(1)} all-to-all(f32[8,512,128]{2,1,0:T(8,128)} %bitcast.9), channel_id=1, replica_groups=mesh['yl'=2,'z'=8,'c'=2,'x'=4,'yh'=2] {'x','yh'}, dimensions={0} | all-to-all | bytes 4194304 | tf_op jit(solution)/shard_map/all_to_all | solution.py:291
  34.7 2.7 %gram.1 = (f32[18,128,128]{2,1,0:T(8,128)S(1)}, f32[18,128,128]{2,1,0:T(8,128)S(1)}, bf16[8,512,256]{2,1,0:T(8,128)(2,1)S(1)}) custom-call(f32[8,512,128]{2,1,0:T(8,128)S(1)} %all_to_all.28.x_ref), custom_call_target="tpu_custom_call" | custom-call | tf_op jit(solution)/shard_map/gram/pallas_call | solution.py:247
  37.4 2.6 %collective-permute-start = (f32[18,128,128]{2,1,0:T(8,128)S(1)}, f32[18,128,128]{2,1,0:T(8,128)S(1)}, u32[]{:S(2)}, u32[]{:S(2)}) collective-permute-start(f32[18,128,128]{2,1,0:T(8,128)S(1)} %get-tuple-element.8), channel_id=1, source_target_pairs={{0,8},{8,0},{1,9},{9,1},{2,10},{10,2},{3,11},{11,3},{4,12},{12,4},... | collective-permute-start | bytes 3538952 | tf_op jit(solution)/shard_map/ppermute | solution.py:285
  40.0 2.5 %collective-permute-done = f32[18,128,128]{2,1,0:T(8,128)S(1)} collective-permute-done((f32[18,128,128]{2,1,0:T(8,128)S(1)}, f32[18,128,128]{2,1,0:T(8,128)S(1)}, u32[]{:S(2)}, u32[]{:S(2)}) %collective-permute-start) | collective-permute-done | bytes 1179680 | tf_op jit(solution)/shard_map/ppermute | solution.py:285
  42.4 0.1 add.12
  42.6 21.0 %all_to_all.29 = f32[16,144,128]{2,1,0:T(8,128)S(1)} all-to-all(f32[16,144,128]{2,1,0:T(8,128)S(1)} %bitcast.8), channel_id=1, replica_groups=mesh['yl'=2,'z'=8,'c'=2,'x'=4,'yh'=2] {'yl','x','yh'}, dimensions={0} | all-to-all | bytes 2359296 | tf_op jit(solution)/shard_map/all_to_all | solution.py:294
  63.6 0.1 reduce_sum.9
  63.7 1.7 collective-permute-start.1
  65.4 1.7 %collective-permute-done.1 = f32[144,128]{1,0:T(8,128)S(1)} collective-permute-done((f32[144,128]{1,0:T(8,128)S(1)}, f32[144,128]{1,0:T(8,128)S(1)}, u32[]{:S(2)}, u32[]{:S(2)}) %collective-permute-start.1) | collective-permute-done | bytes 73760 | tf_op jit(solution)/shard_map/ppermute | solution.py:285
  67.1 3.1 %collective-permute-start.2 = (f32[144,128]{1,0:T(8,128)S(1)}, f32[144,128]{1,0:T(8,128)S(1)}, u32[]{:S(2)}, u32[]{:S(2)}) collective-permute-start(f32[144,128]{1,0:T(8,128)S(1)} %add.13), channel_id=1, source_target_pairs={{0,32},{16,48},{32,0},{48,16},{64,96},{80,112},{96,64},{112,80},{1... | collective-permute-start | bytes 221192 | tf_op jit(solution)/shard_map/ppermute | solution.py:285
  70.2 1.7 %collective-permute-done.2 = f32[144,128]{1,0:T(8,128)S(1)} collective-permute-done((f32[144,128]{1,0:T(8,128)S(1)}, f32[144,128]{1,0:T(8,128)S(1)}, u32[]{:S(2)}, u32[]{:S(2)}) %collective-permute-start.2) | collective-permute-done | bytes 73760 | tf_op jit(solution)/shard_map/ppermute | solution.py:285
  72.0 5.6 %collective-permute-start.3 = (f32[144,128]{1,0:T(8,128)S(1)}, f32[144,128]{1,0:T(8,128)S(1)}, u32[]{:S(2)}, u32[]{:S(2)}) collective-permute-start(f32[144,128]{1,0:T(8,128)S(1)} %add.14), channel_id=1, source_target_pairs={{0,112},{16,96},{32,80},{48,64},{64,48},{80,32},{96,16},{112,0},{1... | collective-permute-start | bytes 221192 | tf_op jit(solution)/shard_map/ppermute | solution.py:285
  77.6 2.3 %collective-permute-done.3 = f32[144,128]{1,0:T(8,128)S(1)} collective-permute-done((f32[144,128]{1,0:T(8,128)S(1)}, f32[144,128]{1,0:T(8,128)S(1)}, u32[]{:S(2)}, u32[]{:S(2)}) %collective-permute-start.3) | collective-permute-done | bytes 73760 | tf_op jit(solution)/shard_map/ppermute | solution.py:285
  79.9 0.1 broadcast_in_dim.2
  80.0 17.0 %all_to_all.30 = f32[16,144,128]{2,1,0:T(8,128)S(1)} all-to-all(f32[16,144,128]{2,1,0:T(8,128)S(1)} %broadcast_in_dim.2), channel_id=1, replica_groups=mesh['yl'=2,'z'=8,'c'=2,'x'=4,'yh'=2] {'yl','x','yh'}, dimensions={0} | all-to-all | bytes 2359296 | tf_op jit(solution)/shard_map/all_to_all | solution.py:298
  97.0 5.7 %collective-permute-start.4 = (f32[18,128,128]{2,1,0:T(8,128)S(1)}, f32[18,128,128]{2,1,0:T(8,128)S(1)}, u32[]{:S(2)}, u32[]{:S(2)}) collective-permute-start(f32[18,128,128]{2,1,0:T(8,128)S(1)} %bitcast.5), channel_id=1, source_target_pairs={{0,8},{8,0},{1,9},{9,1},{2,10},{10,2},{3,11},{11,3},{4,12},{12,4},... | collective-permute-start | bytes 3538952 | tf_op jit(solution)/shard_map/ppermute | solution.py:285
  102.7 2.5 %collective-permute-done.4.other_ref = f32[18,128,128]{2,1,0:T(8,128)S(1)} collective-permute-done((f32[18,128,128]{2,1,0:T(8,128)S(1)}, f32[18,128,128]{2,1,0:T(8,128)S(1)}, u32[]{:S(2)}, u32[]{:S(2)}) %collective-permute-start.4) | collective-permute-done | bytes 1179680 | tf_op jit(solution)/shard_map/ppermute | solution.py:285
  105.2 37.0 %chain.1 = (f32[8,512,128]{2,1,0:T(8,128)S(1)}, f32[1,128]{1,0:T(1,128)}) custom-call(f32[18,128,128]{2,1,0:T(8,128)S(1)} %bitcast.6, f32[18,128,128]{2,1,0:T(8,128)S(1)} %collective-permute-done.4.other_ref, bf16[8,512,256]{2,1,0:T(8,128)(2,1)S(1)} %get-tuple-element.9.x_ref), custom_call_target="tpu_custom_call" | custom-call | tf_op jit(solution)/shard_map/chain/pallas_call | solution.py:261
  142.2 29.9 %all_to_all.31 = f32[8,512,128]{2,1,0:T(8,128)S(1)} all-to-all(f32[8,512,128]{2,1,0:T(8,128)S(1)} %get-tuple-element.10), channel_id=1, replica_groups=mesh['yl'=2,'z'=8,'c'=2,'x'=4,'yh'=2] {'x','yh'}, dimensions={0} | all-to-all | bytes 4194304 | tf_op jit(solution)/shard_map/all_to_all | solution.py:301
  172.1 1.3 copy.4
  (3 shorter events, 0.0 us)
Async XLA Ops:
  37.4 5.0 %collective-permute-start = (f32[18,128,128]{2,1,0:T(8,128)S(1)}, f32[18,128,128]{2,1,0:T(8,128)S(1)}, u32[]{:S(2)}, u32[]{:S(2)}) collective-permute-start(f32[18,128,128]{2,1,0:T(8,128)S(1)} %get-tuple-element.8), channel_id=1, source_target_pairs={{0,8},{8,0},{1,9},{9,1},{2,10},{10,2},{3,11},{11,3},{4,12},{12,4},... | collective-permute-start | bytes 3538952 | tf_op jit(solution)/shard_map/ppermute | solution.py:285
  63.7 3.5 %collective-permute-start.1 = (f32[144,128]{1,0:T(8,128)S(1)}, f32[144,128]{1,0:T(8,128)S(1)}, u32[]{:S(2)}, u32[]{:S(2)}) collective-permute-start(f32[144,128]{1,0:T(8,128)S(1)} %reduce_sum.9), channel_id=1, source_target_pairs={{0,16},{16,0},{32,48},{48,32},{64,80},{80,64},{96,112},{112,96},{1... | collective-permute-start | bytes 221192 | tf_op jit(solution)/shard_map/ppermute | solution.py:285
  67.1 4.8 %collective-permute-start.2 = (f32[144,128]{1,0:T(8,128)S(1)}, f32[144,128]{1,0:T(8,128)S(1)}, u32[]{:S(2)}, u32[]{:S(2)}) collective-permute-start(f32[144,128]{1,0:T(8,128)S(1)} %add.13), channel_id=1, source_target_pairs={{0,32},{16,48},{32,0},{48,16},{64,96},{80,112},{96,64},{112,80},{1... | collective-permute-start | bytes 221192 | tf_op jit(solution)/shard_map/ppermute | solution.py:285
  72.0 7.9 %collective-permute-start.3 = (f32[144,128]{1,0:T(8,128)S(1)}, f32[144,128]{1,0:T(8,128)S(1)}, u32[]{:S(2)}, u32[]{:S(2)}) collective-permute-start(f32[144,128]{1,0:T(8,128)S(1)} %add.14), channel_id=1, source_target_pairs={{0,112},{16,96},{32,80},{48,64},{64,48},{80,32},{96,16},{112,0},{1... | collective-permute-start | bytes 221192 | tf_op jit(solution)/shard_map/ppermute | solution.py:285
  97.0 8.2 %collective-permute-start.4 = (f32[18,128,128]{2,1,0:T(8,128)S(1)}, f32[18,128,128]{2,1,0:T(8,128)S(1)}, u32[]{:S(2)}, u32[]{:S(2)}) collective-permute-start(f32[18,128,128]{2,1,0:T(8,128)S(1)} %bitcast.5), channel_id=1, source_target_pairs={{0,8},{8,0},{1,9},{9,1},{2,10},{10,2},{3,11},{11,3},{4,12},{12,4},... | collective-permute-start | bytes 3538952 | tf_op jit(solution)/shard_map/ppermute | solution.py:285

commit v6 on v5

--- a/solution.py
+++ b/solution.py
@@ -19,7 +19,7 @@
 BF16 = jnp.bfloat16
 MIB = 1024 * 1024
 DOUBLINGS = 4
-GROUP = 4
+GROUP = 8
 
 MOVED = {0: 0, 1: 2, 2 * PAIRS - 2: 2 * PAIRS - 1}
 for place in range(1, PAIRS - 1):
@@ -208,23 +208,10 @@
 
                 @pl.when(trip == t)
                 def _():
+                    now = after if odd else data if t else x_ref
+                    if 2 * t + odd < STEPS - 1:
+                        rotate_data(now, data if odd else after)
                     rotate_gram(lists[2 * t + odd])
-
-            if odd == 0:
-
-                @pl.when(trip == 0)
-                def _():
-                    rotate_data(x_ref, after)
-
-                @pl.when(trip > 0)
-                def _():
-                    rotate_data(data, after)
-
-            else:
-
-                @pl.when(trip < STEPS // 2 - 1)
-                def _():
-                    rotate_data(after, data)
 
         return carry
 
@@ -292,8 +279,9 @@
     keep, send, x = local_gram(x)
     part = (keep + swapped(send, "c", 1)).reshape(sharers, -1, WIDE)
     part = jnp.sum(lax.all_to_all(part, PLANE_AXES, 0, 0, tiled=True), axis=0)
-    for by in (1, 2, 7):
-        part = part + swapped(part, "z", by)
+    near, far, across = (swapped(part, "z", by) for by in (1, 2, 3))
+    part = (part + near) + (far + across)
+    part = part + swapped(part, "z", 7)
     part = jnp.broadcast_to(part[None], (sharers,) + part.shape)
     mine = lax.all_to_all(part, PLANE_AXES, 0, 0, tiled=True).reshape(SHARE, WIDE, WIDE)
     other = swapped(mine, "c", 1)

time: 175 us -> 176 us (level)
  starting transfers between devices: 18.7 us -> 15.5 us
  blocking collectives: 102 us -> 104 us
  Pallas kernels: 39.7 us -> 41.6 us
    ppermute x5 -> x6, starting transfers between devices: 18.7 us -> 15.5 us  [swapped(): lax.ppermute(x, axis, [(i, i ^ by) for i in range(lax.axis_size(axis))])]
    all_to_all x1, blocking collectives: 17 us -> 19.2 us  [body(): lax.all_to_all(part, PLANE_AXES, 0, 0, tiled=True)]
    pallas_call x1, Pallas kernels: 37 us -> 38.9 us  [chain(): pl.pallas_call(chain_kernel, out_shape=(jax.ShapeDtypeStruct((PAIRS, rows...]
    ppermute x5 -> x6, waiting for transfers between devices: 10.7 us -> 12.2 us  [swapped(): lax.ppermute(x, axis, [(i, i ^ by) for i in range(lax.axis_size(axis))])]
  transfers between devices with their start and end apart: 5 -> 6, of which waited for: 5 -> 5; matrix products, arithmetic and copies ran while one was open for 0% -> 0% of each run, Pallas kernels for 0% -> 0%
where the time goes in v6:
time: 176 us; the launch traced here: 175 us
  blocking collectives  104 us (59%)
  Pallas kernels  41.6 us (24%)
  starting transfers between devices  15.5 us (9%)
  waiting for transfers between devices  12.2 us (7%)
    pallas_call x1, Pallas kernels, chain(): pl.pallas_call(chain_kernel, out_shape=(jax.ShapeDtypeStruct((PAIRS, rows...  38.9 us
    all_to_all x1, blocking collectives, body(): lax.all_to_all(snapshots, PAIR_AXES, 0, 0, tiled=True)  34.1 us
    all_to_all x1, blocking collectives, body(): lax.all_to_all(y.reshape(snapshots.shape), PAIR_AXES, 0, 0, tiled=True)  29.3 us
    all_to_all x1, blocking collectives, body(): part = jnp.sum(lax.all_to_all(part, PLANE_AXES, 0, 0, tiled=True), axis=0)  21 us
    all_to_all x1, blocking collectives, body(): lax.all_to_all(part, PLANE_AXES, 0, 0, tiled=True)  19.2 us
    ppermute x6, starting transfers between devices, swapped(): lax.ppermute(x, axis, [(i, i ^ by) for i in range(lax.axis_size(axis))])  15.5 us
    ppermute x6, waiting for transfers between devices, swapped(): lax.ppermute(x, axis, [(i, i ^ by) for i in range(lax.axis_size(axis))])  12.2 us
  transfers between devices with their start and end apart: 6, of which 5 were waited for; matrix products, arithmetic and copies ran while one was open for 0% of the time, Pallas kernels for 0%

profile of v6, /device:TPU:1, one launch (start us, length us, event | category | flops | bytes accessed | tf_op | source)
XLA Modules:
  0.0 175.2 jit_solution(7982679576244086287)
XLA Ops:
  0.6 34.1 %all_to_all.28.x_ref = f32[8,512,128]{2,1,0:T(8,128)S(1)} all-to-all(f32[8,512,128]{2,1,0:T(8,128)} %bitcast.9), channel_id=1, replica_groups=mesh['yl'=2,'z'=8,'c'=2,'x'=4,'yh'=2] {'x','yh'}, dimensions={0} | all-to-all | bytes 4194304 | tf_op jit(solution)/shard_map/all_to_all | solution.py:278
  34.7 2.7 %gram.1 = (f32[18,128,128]{2,1,0:T(8,128)S(1)}, f32[18,128,128]{2,1,0:T(8,128)S(1)}, bf16[8,512,256]{2,1,0:T(8,128)(2,1)S(1)}) custom-call(f32[8,512,128]{2,1,0:T(8,128)S(1)} %all_to_all.28.x_ref), custom_call_target="tpu_custom_call" | custom-call | tf_op jit(solution)/shard_map/gram/pallas_call | solution.py:234
  37.4 2.6 %collective-permute-start = (f32[18,128,128]{2,1,0:T(8,128)S(1)}, f32[18,128,128]{2,1,0:T(8,128)S(1)}, u32[]{:S(2)}, u32[]{:S(2)}) collective-permute-start(f32[18,128,128]{2,1,0:T(8,128)S(1)} %get-tuple-element.8), channel_id=1, source_target_pairs={{0,8},{8,0},{1,9},{9,1},{2,10},{10,2},{3,11},{11,3},{4,12},{12,4},... | collective-permute-start | bytes 3538952 | tf_op jit(solution)/shard_map/ppermute | solution.py:272
  40.0 2.5 %collective-permute-done = f32[18,128,128]{2,1,0:T(8,128)S(1)} collective-permute-done((f32[18,128,128]{2,1,0:T(8,128)S(1)}, f32[18,128,128]{2,1,0:T(8,128)S(1)}, u32[]{:S(2)}, u32[]{:S(2)}) %collective-permute-start) | collective-permute-done | bytes 1179680 | tf_op jit(solution)/shard_map/ppermute | solution.py:272
  42.4 0.1 add.15
  42.6 21.0 %all_to_all.29 = f32[16,144,128]{2,1,0:T(8,128)S(1)} all-to-all(f32[16,144,128]{2,1,0:T(8,128)S(1)} %bitcast.8), channel_id=1, replica_groups=mesh['yl'=2,'z'=8,'c'=2,'x'=4,'yh'=2] {'yl','x','yh'}, dimensions={0} | all-to-all | bytes 2359296 | tf_op jit(solution)/shard_map/all_to_all | solution.py:281
  63.6 0.1 reduce_sum.9
  63.7 4.4 %collective-permute-start.3 = (f32[144,128]{1,0:T(8,128)S(1)}, f32[144,128]{1,0:T(8,128)S(1)}, u32[]{:S(2)}, u32[]{:S(2)}) collective-permute-start(f32[144,128]{1,0:T(8,128)S(1)} %reduce_sum.9), channel_id=1, source_target_pairs={{0,48},{16,32},{32,16},{48,0},{64,112},{80,96},{96,80},{112,64},{1... | collective-permute-start | bytes 221192 | tf_op jit(solution)/shard_map/ppermute | solution.py:272
  68.1 0.0 collective-permute-start.2
  68.1 0.4 collective-permute-start.1
  68.5 1.4 collective-permute-done.3
  69.9 3.9 %collective-permute-done.2 = f32[144,128]{1,0:T(8,128)S(1)} collective-permute-done((f32[144,128]{1,0:T(8,128)S(1)}, f32[144,128]{1,0:T(8,128)S(1)}, u32[]{:S(2)}, u32[]{:S(2)}) %collective-permute-start.2) | collective-permute-done | bytes 73760 | tf_op jit(solution)/shard_map/ppermute | solution.py:272
  73.8 0.0 collective-permute-done.1
  73.8 4.6 %collective-permute-start.4 = (f32[144,128]{1,0:T(8,128)S(1)}, f32[144,128]{1,0:T(8,128)S(1)}, u32[]{:S(2)}, u32[]{:S(2)}) collective-permute-start(f32[144,128]{1,0:T(8,128)S(1)} %add_add_fusion), channel_id=1, source_target_pairs={{0,112},{16,96},{32,80},{48,64},{64,48},{80,32},{96,16},{112,0},{1... | collective-permute-start | bytes 221192 | tf_op jit(solution)/shard_map/ppermute | solution.py:272
  78.4 2.0 %collective-permute-done.4 = f32[144,128]{1,0:T(8,128)S(1)} collective-permute-done((f32[144,128]{1,0:T(8,128)S(1)}, f32[144,128]{1,0:T(8,128)S(1)}, u32[]{:S(2)}, u32[]{:S(2)}) %collective-permute-start.4) | collective-permute-done | bytes 73760 | tf_op jit(solution)/shard_map/ppermute | solution.py:272
  80.4 0.1 broadcast_in_dim.2
  80.5 19.2 %all_to_all.30 = f32[16,144,128]{2,1,0:T(8,128)S(1)} all-to-all(f32[16,144,128]{2,1,0:T(8,128)S(1)} %broadcast_in_dim.2), channel_id=1, replica_groups=mesh['yl'=2,'z'=8,'c'=2,'x'=4,'yh'=2] {'yl','x','yh'}, dimensions={0} | all-to-all | bytes 2359296 | tf_op jit(solution)/shard_map/all_to_all | solution.py:286
  99.7 3.5 %collective-permute-start.5 = (f32[18,128,128]{2,1,0:T(8,128)S(1)}, f32[18,128,128]{2,1,0:T(8,128)S(1)}, u32[]{:S(2)}, u32[]{:S(2)}) collective-permute-start(f32[18,128,128]{2,1,0:T(8,128)S(1)} %bitcast.5), channel_id=1, source_target_pairs={{0,8},{8,0},{1,9},{9,1},{2,10},{10,2},{3,11},{11,3},{4,12},{12,4},... | collective-permute-start | bytes 3538952 | tf_op jit(solution)/shard_map/ppermute | solution.py:272
  103.2 2.5 %collective-permute-done.5.other_ref = f32[18,128,128]{2,1,0:T(8,128)S(1)} collective-permute-done((f32[18,128,128]{2,1,0:T(8,128)S(1)}, f32[18,128,128]{2,1,0:T(8,128)S(1)}, u32[]{:S(2)}, u32[]{:S(2)}) %collective-permute-start.5) | collective-permute-done | bytes 1179680 | tf_op jit(solution)/shard_map/ppermute | solution.py:272
  105.7 38.9 %chain.1 = (f32[8,512,128]{2,1,0:T(8,128)S(1)}, f32[1,128]{1,0:T(1,128)}) custom-call(f32[18,128,128]{2,1,0:T(8,128)S(1)} %bitcast.6, f32[18,128,128]{2,1,0:T(8,128)S(1)} %collective-permute-done.5.other_ref, bf16[8,512,256]{2,1,0:T(8,128)(2,1)S(1)} %get-tuple-element.9.x_ref), custom_call_target="tpu_custom_call" | custom-call | tf_op jit(solution)/shard_map/chain/pallas_call | solution.py:248
  144.6 29.3 %all_to_all.31 = f32[8,512,128]{2,1,0:T(8,128)S(1)} all-to-all(f32[8,512,128]{2,1,0:T(8,128)S(1)} %get-tuple-element.10), channel_id=1, replica_groups=mesh['yl'=2,'z'=8,'c'=2,'x'=4,'yh'=2] {'x','yh'}, dimensions={0} | all-to-all | bytes 4194304 | tf_op jit(solution)/shard_map/all_to_all | solution.py:289
  173.9 1.3 copy.4
  (2 shorter events, 0.0 us)
Async XLA Ops:
  37.4 5.0 %collective-permute-start = (f32[18,128,128]{2,1,0:T(8,128)S(1)}, f32[18,128,128]{2,1,0:T(8,128)S(1)}, u32[]{:S(2)}, u32[]{:S(2)}) collective-permute-start(f32[18,128,128]{2,1,0:T(8,128)S(1)} %get-tuple-element.8), channel_id=1, source_target_pairs={{0,8},{8,0},{1,9},{9,1},{2,10},{10,2},{3,11},{11,3},{4,12},{12,4},... | collective-permute-start | bytes 3538952 | tf_op jit(solution)/shard_map/ppermute | solution.py:272
  63.7 6.2 %collective-permute-start.3 = (f32[144,128]{1,0:T(8,128)S(1)}, f32[144,128]{1,0:T(8,128)S(1)}, u32[]{:S(2)}, u32[]{:S(2)}) collective-permute-start(f32[144,128]{1,0:T(8,128)S(1)} %reduce_sum.9), channel_id=1, source_target_pairs={{0,48},{16,32},{32,16},{48,0},{64,112},{80,96},{96,80},{112,64},{1... | collective-permute-start | bytes 221192 | tf_op jit(solution)/shard_map/ppermute | solution.py:272
  68.1 5.7 %collective-permute-start.2 = (f32[144,128]{1,0:T(8,128)S(1)}, f32[144,128]{1,0:T(8,128)S(1)}, u32[]{:S(2)}, u32[]{:S(2)}) collective-permute-start(f32[144,128]{1,0:T(8,128)S(1)} %reduce_sum.9), channel_id=1, source_target_pairs={{0,32},{16,48},{32,0},{48,16},{64,96},{80,112},{96,64},{112,80},{1... | collective-permute-start | bytes 221192 | tf_op jit(solution)/shard_map/ppermute | solution.py:272
  68.1 5.7 %collective-permute-start.1 = (f32[144,128]{1,0:T(8,128)S(1)}, f32[144,128]{1,0:T(8,128)S(1)}, u32[]{:S(2)}, u32[]{:S(2)}) collective-permute-start(f32[144,128]{1,0:T(8,128)S(1)} %reduce_sum.9), channel_id=1, source_target_pairs={{0,16},{16,0},{32,48},{48,32},{64,80},{80,64},{96,112},{112,96},{1... | collective-permute-start | bytes 221192 | tf_op jit(solution)/shard_map/ppermute | solution.py:272
  73.8 6.6 %collective-permute-start.4 = (f32[144,128]{1,0:T(8,128)S(1)}, f32[144,128]{1,0:T(8,128)S(1)}, u32[]{:S(2)}, u32[]{:S(2)}) collective-permute-start(f32[144,128]{1,0:T(8,128)S(1)} %add_add_fusion), channel_id=1, source_target_pairs={{0,112},{16,96},{32,80},{48,64},{64,48},{80,32},{96,16},{112,0},{1... | collective-permute-start | bytes 221192 | tf_op jit(solution)/shard_map/ppermute | solution.py:272
  99.7 6.0 %collective-permute-start.5 = (f32[18,128,128]{2,1,0:T(8,128)S(1)}, f32[18,128,128]{2,1,0:T(8,128)S(1)}, u32[]{:S(2)}, u32[]{:S(2)}) collective-permute-start(f32[18,128,128]{2,1,0:T(8,128)S(1)} %bitcast.5), channel_id=1, source_target_pairs={{0,8},{8,0},{1,9},{9,1},{2,10},{10,2},{3,11},{11,3},{4,12},{12,4},... | collective-permute-start | bytes 3538952 | tf_op jit(solution)/shard_map/ppermute | solution.py:272

commit v7 on v6

--- a/solution.py
+++ b/solution.py
@@ -281,7 +281,7 @@
     part = jnp.sum(lax.all_to_all(part, PLANE_AXES, 0, 0, tiled=True), axis=0)
     near, far, across = (swapped(part, "z", by) for by in (1, 2, 3))
     part = (part + near) + (far + across)
-    part = part + swapped(part, "z", 7)
+    part = part + swapped(part, "z", 6)
     part = jnp.broadcast_to(part[None], (sharers,) + part.shape)
     mine = lax.all_to_all(part, PLANE_AXES, 0, 0, tiled=True).reshape(SHARE, WIDE, WIDE)
     other = swapped(mine, "c", 1)

time: 176 us -> 177 us (level)
  no operation moved by 1% of the time
where the time goes in v7:
time: 177 us; the launch traced here: 175 us
  blocking collectives  105 us (59%)
  Pallas kernels  41.6 us (24%)
  starting transfers between devices  13.8 us (8%)
  waiting for transfers between devices  12.6 us (7%)
    pallas_call x1, Pallas kernels, chain(): pl.pallas_call(chain_kernel, out_shape=(jax.ShapeDtypeStruct((PAIRS, rows...  38.9 us
    all_to_all x1, blocking collectives, body(): lax.all_to_all(snapshots, PAIR_AXES, 0, 0, tiled=True)  34.1 us
    all_to_all x1, blocking collectives, body(): lax.all_to_all(y.reshape(snapshots.shape), PAIR_AXES, 0, 0, tiled=True)  29.7 us
    all_to_all x1, blocking collectives, body(): part = jnp.sum(lax.all_to_all(part, PLANE_AXES, 0, 0, tiled=True), axis=0)  21 us
    all_to_all x1, blocking collectives, body(): lax.all_to_all(part, PLANE_AXES, 0, 0, tiled=True)  19.9 us
    ppermute x6, starting transfers between devices, swapped(): lax.ppermute(x, axis, [(i, i ^ by) for i in range(lax.axis_size(axis))])  13.8 us
    ppermute x6, waiting for transfers between devices, swapped(): lax.ppermute(x, axis, [(i, i ^ by) for i in range(lax.axis_size(axis))])  12.6 us
  transfers between devices with their start and end apart: 6, of which 5 were waited for; matrix products, arithmetic and copies ran while one was open for 0% of the time, Pallas kernels for 0%

profile of v7, /device:TPU:1, one launch (start us, length us, event | category | flops | bytes accessed | tf_op | source)
XLA Modules:
  0.0 174.9 jit_solution(7458531747764389662)
XLA Ops:
  0.6 34.1 %all_to_all.28.x_ref = f32[8,512,128]{2,1,0:T(8,128)S(1)} all-to-all(f32[8,512,128]{2,1,0:T(8,128)} %bitcast.9), channel_id=1, replica_groups=mesh['yl'=2,'z'=8,'c'=2,'x'=4,'yh'=2] {'x','yh'}, dimensions={0} | all-to-all | bytes 4194304 | tf_op jit(solution)/shard_map/all_to_all | solution.py:278
  34.7 2.7 %gram.1 = (f32[18,128,128]{2,1,0:T(8,128)S(1)}, f32[18,128,128]{2,1,0:T(8,128)S(1)}, bf16[8,512,256]{2,1,0:T(8,128)(2,1)S(1)}) custom-call(f32[8,512,128]{2,1,0:T(8,128)S(1)} %all_to_all.28.x_ref), custom_call_target="tpu_custom_call" | custom-call | tf_op jit(solution)/shard_map/gram/pallas_call | solution.py:234
  37.4 2.6 %collective-permute-start = (f32[18,128,128]{2,1,0:T(8,128)S(1)}, f32[18,128,128]{2,1,0:T(8,128)S(1)}, u32[]{:S(2)}, u32[]{:S(2)}) collective-permute-start(f32[18,128,128]{2,1,0:T(8,128)S(1)} %get-tuple-element.8), channel_id=1, source_target_pairs={{0,8},{8,0},{1,9},{9,1},{2,10},{10,2},{3,11},{11,3},{4,12},{12,4},... | collective-permute-start | bytes 3538952 | tf_op jit(solution)/shard_map/ppermute | solution.py:272
  40.0 2.5 %collective-permute-done = f32[18,128,128]{2,1,0:T(8,128)S(1)} collective-permute-done((f32[18,128,128]{2,1,0:T(8,128)S(1)}, f32[18,128,128]{2,1,0:T(8,128)S(1)}, u32[]{:S(2)}, u32[]{:S(2)}) %collective-permute-start) | collective-permute-done | bytes 1179680 | tf_op jit(solution)/shard_map/ppermute | solution.py:272
  42.4 0.1 add.15
  42.6 21.0 %all_to_all.29 = f32[16,144,128]{2,1,0:T(8,128)S(1)} all-to-all(f32[16,144,128]{2,1,0:T(8,128)S(1)} %bitcast.8), channel_id=1, replica_groups=mesh['yl'=2,'z'=8,'c'=2,'x'=4,'yh'=2] {'yl','x','yh'}, dimensions={0} | all-to-all | bytes 2359296 | tf_op jit(solution)/shard_map/all_to_all | solution.py:281
  63.6 0.1 reduce_sum.9
  63.7 4.4 %collective-permute-start.3 = (f32[144,128]{1,0:T(8,128)S(1)}, f32[144,128]{1,0:T(8,128)S(1)}, u32[]{:S(2)}, u32[]{:S(2)}) collective-permute-start(f32[144,128]{1,0:T(8,128)S(1)} %reduce_sum.9), channel_id=1, source_target_pairs={{0,48},{16,32},{32,16},{48,0},{64,112},{80,96},{96,80},{112,64},{1... | collective-permute-start | bytes 221192 | tf_op jit(solution)/shard_map/ppermute | solution.py:272
  68.1 0.0 collective-permute-start.2
  68.1 0.4 collective-permute-start.1
  68.5 1.4 collective-permute-done.3
  69.9 3.9 %collective-permute-done.2 = f32[144,128]{1,0:T(8,128)S(1)} collective-permute-done((f32[144,128]{1,0:T(8,128)S(1)}, f32[144,128]{1,0:T(8,128)S(1)}, u32[]{:S(2)}, u32[]{:S(2)}) %collective-permute-start.2) | collective-permute-done | bytes 73760 | tf_op jit(solution)/shard_map/ppermute | solution.py:272
  73.8 0.0 collective-permute-done.1
  73.8 3.4 %collective-permute-start.4 = (f32[144,128]{1,0:T(8,128)S(1)}, f32[144,128]{1,0:T(8,128)S(1)}, u32[]{:S(2)}, u32[]{:S(2)}) collective-permute-start(f32[144,128]{1,0:T(8,128)S(1)} %add_add_fusion), channel_id=1, source_target_pairs={{0,96},{16,112},{32,64},{48,80},{64,32},{80,48},{96,0},{112,16},{1... | collective-permute-start | bytes 221192 | tf_op jit(solution)/shard_map/ppermute | solution.py:272
  77.2 2.4 %collective-permute-done.4 = f32[144,128]{1,0:T(8,128)S(1)} collective-permute-done((f32[144,128]{1,0:T(8,128)S(1)}, f32[144,128]{1,0:T(8,128)S(1)}, u32[]{:S(2)}, u32[]{:S(2)}) %collective-permute-start.4) | collective-permute-done | bytes 73760 | tf_op jit(solution)/shard_map/ppermute | solution.py:272
  79.6 0.1 broadcast_in_dim.2
  79.7 19.9 %all_to_all.30 = f32[16,144,128]{2,1,0:T(8,128)S(1)} all-to-all(f32[16,144,128]{2,1,0:T(8,128)S(1)} %broadcast_in_dim.2), channel_id=1, replica_groups=mesh['yl'=2,'z'=8,'c'=2,'x'=4,'yh'=2] {'yl','x','yh'}, dimensions={0} | all-to-all | bytes 2359296 | tf_op jit(solution)/shard_map/all_to_all | solution.py:286
  99.6 3.0 %collective-permute-start.5 = (f32[18,128,128]{2,1,0:T(8,128)S(1)}, f32[18,128,128]{2,1,0:T(8,128)S(1)}, u32[]{:S(2)}, u32[]{:S(2)}) collective-permute-start(f32[18,128,128]{2,1,0:T(8,128)S(1)} %bitcast.5), channel_id=1, source_target_pairs={{0,8},{8,0},{1,9},{9,1},{2,10},{10,2},{3,11},{11,3},{4,12},{12,4},... | collective-permute-start | bytes 3538952 | tf_op jit(solution)/shard_map/ppermute | solution.py:272
  102.6 2.5 %collective-permute-done.5.other_ref = f32[18,128,128]{2,1,0:T(8,128)S(1)} collective-permute-done((f32[18,128,128]{2,1,0:T(8,128)S(1)}, f32[18,128,128]{2,1,0:T(8,128)S(1)}, u32[]{:S(2)}, u32[]{:S(2)}) %collective-permute-start.5) | collective-permute-done | bytes 1179680 | tf_op jit(solution)/shard_map/ppermute | solution.py:272
  105.1 38.9 %chain.1 = (f32[8,512,128]{2,1,0:T(8,128)S(1)}, f32[1,128]{1,0:T(1,128)}) custom-call(f32[18,128,128]{2,1,0:T(8,128)S(1)} %bitcast.6, f32[18,128,128]{2,1,0:T(8,128)S(1)} %collective-permute-done.5.other_ref, bf16[8,512,256]{2,1,0:T(8,128)(2,1)S(1)} %get-tuple-element.9.x_ref), custom_call_target="tpu_custom_call" | custom-call | tf_op jit(solution)/shard_map/chain/pallas_call | solution.py:248
  143.9 29.7 %all_to_all.31 = f32[8,512,128]{2,1,0:T(8,128)S(1)} all-to-all(f32[8,512,128]{2,1,0:T(8,128)S(1)} %get-tuple-element.10), channel_id=1, replica_groups=mesh['yl'=2,'z'=8,'c'=2,'x'=4,'yh'=2] {'x','yh'}, dimensions={0} | all-to-all | bytes 4194304 | tf_op jit(solution)/shard_map/all_to_all | solution.py:289
  173.6 1.3 copy.4
  (2 shorter events, 0.0 us)
Async XLA Ops:
  37.4 5.0 %collective-permute-start = (f32[18,128,128]{2,1,0:T(8,128)S(1)}, f32[18,128,128]{2,1,0:T(8,128)S(1)}, u32[]{:S(2)}, u32[]{:S(2)}) collective-permute-start(f32[18,128,128]{2,1,0:T(8,128)S(1)} %get-tuple-element.8), channel_id=1, source_target_pairs={{0,8},{8,0},{1,9},{9,1},{2,10},{10,2},{3,11},{11,3},{4,12},{12,4},... | collective-permute-start | bytes 3538952 | tf_op jit(solution)/shard_map/ppermute | solution.py:272
  63.7 6.2 %collective-permute-start.3 = (f32[144,128]{1,0:T(8,128)S(1)}, f32[144,128]{1,0:T(8,128)S(1)}, u32[]{:S(2)}, u32[]{:S(2)}) collective-permute-start(f32[144,128]{1,0:T(8,128)S(1)} %reduce_sum.9), channel_id=1, source_target_pairs={{0,48},{16,32},{32,16},{48,0},{64,112},{80,96},{96,80},{112,64},{1... | collective-permute-start | bytes 221192 | tf_op jit(solution)/shard_map/ppermute | solution.py:272
  68.1 5.7 %collective-permute-start.2 = (f32[144,128]{1,0:T(8,128)S(1)}, f32[144,128]{1,0:T(8,128)S(1)}, u32[]{:S(2)}, u32[]{:S(2)}) collective-permute-start(f32[144,128]{1,0:T(8,128)S(1)} %reduce_sum.9), channel_id=1, source_target_pairs={{0,32},{16,48},{32,0},{48,16},{64,96},{80,112},{96,64},{112,80},{1... | collective-permute-start | bytes 221192 | tf_op jit(solution)/shard_map/ppermute | solution.py:272
  68.1 5.7 %collective-permute-start.1 = (f32[144,128]{1,0:T(8,128)S(1)}, f32[144,128]{1,0:T(8,128)S(1)}, u32[]{:S(2)}, u32[]{:S(2)}) collective-permute-start(f32[144,128]{1,0:T(8,128)S(1)} %reduce_sum.9), channel_id=1, source_target_pairs={{0,16},{16,0},{32,48},{48,32},{64,80},{80,64},{96,112},{112,96},{1... | collective-permute-start | bytes 221192 | tf_op jit(solution)/shard_map/ppermute | solution.py:272
  73.8 5.8 %collective-permute-start.4 = (f32[144,128]{1,0:T(8,128)S(1)}, f32[144,128]{1,0:T(8,128)S(1)}, u32[]{:S(2)}, u32[]{:S(2)}) collective-permute-start(f32[144,128]{1,0:T(8,128)S(1)} %add_add_fusion), channel_id=1, source_target_pairs={{0,96},{16,112},{32,64},{48,80},{64,32},{80,48},{96,0},{112,16},{1... | collective-permute-start | bytes 221192 | tf_op jit(solution)/shard_map/ppermute | solution.py:272
  99.6 5.5 %collective-permute-start.5 = (f32[18,128,128]{2,1,0:T(8,128)S(1)}, f32[18,128,128]{2,1,0:T(8,128)S(1)}, u32[]{:S(2)}, u32[]{:S(2)}) collective-permute-start(f32[18,128,128]{2,1,0:T(8,128)S(1)} %bitcast.5), channel_id=1, source_target_pairs={{0,8},{8,0},{1,9},{9,1},{2,10},{10,2},{3,11},{11,3},{4,12},{12,4},... | collective-permute-start | bytes 3538952 | tf_op jit(solution)/shard_map/ppermute | solution.py:272
